TPU v7x, 256 devices: a whole 4x4x8 slice. The times are simulated.
256 devices in a mesh: group: 16 (over z_hi, y), section: 2 (over z_lo), tensor: 8 (over x, core).
Axes of the slice: x: 4, y: 4, z: 8 (z_hi: 4, z_lo: 2; z = z_hi * 2 + z_lo), core: 2. Of those that a mesh axis runs over, the one named last changes fastest.
Arguments:
- hidden: bfloat16 [2, 64, 4, 8192], P('section', 'group', None, 'tensor'), may hold values from -6 to 6
- base_kv: bfloat16 [16, 8192, 256], P(('section', 'tensor')), may hold values from -0.0625 to 0.0625
- delta_codes: bfloat16 [16, 8192, 256], P(None, ('group', 'section', 'tensor')), may hold values from -448 to 448
- delta_scales: bfloat16 [16, 8192, 2], P(None, ('group', 'section', 'tensor')), may hold values from 1.9907951e-05 to 0.00019931793
- queries: bfloat16 [2, 64, 4, 8192], P('section', 'group', None, 'tensor'), may hold values from -4 to 4
- key_cache: bfloat16 [2, 64, 8, 4096, 128], P('section', 'group', 'tensor'), may hold values from -400 to 400
- value_cache: bfloat16 [2, 64, 8, 4096, 128], P('section', 'group', 'tensor'), may hold values from -6 to 6
- lengths: int32 [64], P('group'), may hold values from 1024 to 4096, as said below
Outputs:
- new_entries: bfloat16 [2, 64, 4, 2048], P('section', 'group', None, 'tensor')
- attended: bfloat16 [2, 64, 4, 8192], P('section', 'group', None, 'tensor')
Inputs may be any that keep to these rules, and one draw needn't show every extreme that they name: `lengths`: some row has exactly 4096 cached positions and some row exactly 1024.
All inputs are finite; a program needn't handle non-finite values.
Results may differ from a plain program's by a relative error of at most 0.005.
Values may be sent and summed in bfloat16 or wider, within the bound.
A program may use at most 128 MiB of HBM per device.

v0:
```python
import math

import jax
import jax.numpy as jnp
from jax import lax
from jax.sharding import PartitionSpec as P


def rotate(key_part, positions):
    half_size = key_part.shape[-1] // 2
    freq_index = jnp.arange(half_size, dtype=jnp.float32)
    frequency = jnp.exp(freq_index * (-2.0 * math.log(1000000.0) / key_part.shape[-1]))
    phases = positions[..., None] * frequency
    cosine = jnp.cos(phases)
    sine_part = jnp.sin(phases)
    first_half = key_part[..., :half_size]
    second_half = key_part[..., half_size:]
    return jnp.concatenate(
        [
            first_half * cosine - second_half * sine_part,
            second_half * cosine + first_half * sine_part,
        ],
        axis=-1,
    )


def dequantize(code_part, scale_part):
    head_size = code_part.shape[-1] // 2
    scale_full = jnp.repeat(scale_part.astype(jnp.float32), head_size, axis=2)
    return (code_part.astype(jnp.float32) * scale_full).astype(jnp.bfloat16)


def reorder(arrived, block_count, replica_count):
    heads_here, row_total, columns = arrived.shape
    owned = row_total // (block_count * replica_count)
    shaped = arrived.reshape(heads_here, block_count, replica_count, owned, columns)
    return jnp.transpose(shaped, (0, 2, 1, 3, 4)).reshape(heads_here, row_total, columns)


def body(hidden, base_kv, delta_codes, delta_scales, queries, key_cache, value_cache, lengths):
    heads_here = base_kv.shape[0]
    model_width = base_kv.shape[1]
    pair_width = base_kv.shape[2]
    head_size = pair_width // 2
    row_count = hidden.shape[1]
    step_count = hidden.shape[2]
    context = key_cache.shape[3]
    group_size = queries.shape[3] // (heads_here * head_size)
    features = lax.all_gather(hidden, "tensor", axis=3, tiled=True)
    inputs = features.reshape(row_count * step_count, model_width)
    base_projected = jnp.einsum("nd,jdc->njc", inputs, base_kv, preferred_element_type=jnp.float32)
    codes_all, scales_all = (
        lax.all_gather(delta_codes, "group", axis=1, tiled=True),
        lax.all_gather(delta_scales, "group", axis=1, tiled=True),
    )
    codes_mine, scales_mine = (
        lax.all_to_all(codes_all, ("section", "tensor"), split_axis=0, concat_axis=1, tiled=True),
        lax.all_to_all(scales_all, ("section", "tensor"), split_axis=0, concat_axis=1, tiled=True),
    )
    block_count = lax.axis_size("section") * lax.axis_size("tensor")
    replica_count = lax.axis_size("group")
    codes_mine = reorder(codes_mine, block_count, replica_count)
    scales_mine = reorder(scales_mine, block_count, replica_count)
    delta_mine = dequantize(codes_mine, scales_mine)
    projected = base_projected + jnp.einsum(
        "nd,jdc->njc", inputs, delta_mine, preferred_element_type=jnp.float32
    )
    projected = projected.reshape(row_count, step_count, heads_here, pair_width)
    offsets = jnp.arange(step_count, dtype=jnp.int32)
    positions = (lengths[:, None] + offsets[None, :]).astype(jnp.float32)
    fresh_keys = rotate(projected[..., :head_size], positions[:, :, None]).astype(jnp.bfloat16)
    fresh_values = projected[..., head_size:].astype(jnp.bfloat16)
    new_entries = jnp.concatenate([fresh_keys, fresh_values], axis=-1).reshape(
        1, row_count, step_count, heads_here * pair_width
    )
    score_scale = head_size ** (-0.5)
    query_block = queries[0].reshape(row_count, step_count, heads_here, group_size, head_size)
    cache_scores = (
        jnp.einsum(
            "rtjgh,rjph->rjtgp", query_block, key_cache[0], preferred_element_type=jnp.float32
        )
        * score_scale
    )
    fresh_scores = (
        jnp.einsum("rtjgh,rujh->rjtgu", query_block, fresh_keys, preferred_element_type=jnp.float32)
        * score_scale
    )
    cache_visible = (jnp.arange(context, dtype=jnp.int32)[None, :] < lengths[:, None])[
        :, None, None, None, :
    ]
    fresh_visible = (offsets[None, :] <= offsets[:, None])[None, None, :, None, :]
    peak_score = jnp.maximum(
        jnp.max(jnp.where(cache_visible, cache_scores, -jnp.inf), axis=-1),
        jnp.max(jnp.where(fresh_visible, fresh_scores, -jnp.inf), axis=-1),
    )
    cache_exp = jnp.where(cache_visible, jnp.exp(cache_scores - peak_score[..., None]), 0.0)
    fresh_exp = jnp.where(fresh_visible, jnp.exp(fresh_scores - peak_score[..., None]), 0.0)
    normaliser = jnp.sum(cache_exp, axis=-1) + jnp.sum(fresh_exp, axis=-1)
    cache_weights = (cache_exp / normaliser[..., None]).astype(jnp.bfloat16)
    fresh_weights = (fresh_exp / normaliser[..., None]).astype(jnp.bfloat16)
    output = jnp.einsum(
        "rjtgp,rjph->rtjgh", cache_weights, value_cache[0], preferred_element_type=jnp.float32
    )
    output = output + jnp.einsum(
        "rjtgu,rujh->rtjgh", fresh_weights, fresh_values, preferred_element_type=jnp.float32
    )
    attended = output.reshape(1, row_count, step_count, heads_here * group_size * head_size).astype(
        jnp.bfloat16
    )
    return (new_entries, attended)


def solution(mesh):
    placed = (
        P("section", "group", None, "tensor"),
        P(("section", "tensor"), None, None),
        P(None, ("group", "section", "tensor"), None),
        P(None, ("group", "section", "tensor"), None),
        P("section", "group", None, "tensor"),
        P("section", "group", "tensor", None, None),
        P("section", "group", "tensor", None, None),
        P("group"),
    )
    return jax.shard_map(
        body,
        mesh=mesh,
        in_specs=placed,
        out_specs=(P("section", "group", None, "tensor"), P("section", "group", None, "tensor")),
        check_vma=False,
    )
```

profile of v0, /device:TPU:7, one launch (start us, length us, event | category | flops | bytes accessed | tf_op | source)
XLA Modules:
  0.0 216.7 jit_solution(5329329909233001848)
XLA Ops:
  7.2 0.0 all-gather.2.cloned.1.call-start
  7.2 0.7 all-gather.2.cloned.1.call-update
  7.9 0.8 copy.18
  8.7 42.5 %all_gather.11 = bf16[16,512,2]{0,2,1:T(2,128)(2,1)S(1)} all-gather(bf16[16,32,2]{0,2,1:T(2,128)(2,1)S(1)} %copy.18), channel_id=1, replica_groups=mesh['group'=16,'section'=2,'tensor'=8] {'group'}, dimensions={1}, use_global_device_ids=true | all-gather | bytes 34816 | tf_op jit(solution)/shard_map/all_gather | solution.py:54
  51.2 0.1 copy.19
  51.3 17.5 %all_to_all.8 = bf16[16,512,2]{1,2,0:T(2,128)(2,1)S(1)} all-to-all(bf16[16,512,2]{1,2,0:T(2,128)(2,1)S(1)} %copy.19), channel_id=1, replica_groups=mesh['group'=16,'section'=2,'tensor'=8] {'section','tensor'}, dimensions={0} | all-to-all | bytes 65536 | tf_op jit(solution)/shard_map/all_to_all | solution.py:58
  68.8 0.0 copy-start.1
  68.8 0.0 copy-start.2
  68.8 0.0 copy-start.3
  68.8 22.7 %all-gather.2.cloned.1.call-done = bf16[16,512,256]{2,1,0:T(8,128)(2,1)} async-done(((bf16[16,32,256]{2,1,0:T(8,128)(2,1)}), bf16[16,512,256]{2,1,0:T(8,128)(2,1)}) %all-gather.2.cloned.1.call-update) | async-done | bytes 4194320 | tf_op jit(solution)/shard_map/all_gather | solution.py:53
  91.5 5.2 %all-to-all-start = ((bf16[16,512,256]{2,1,0:T(8,128)(2,1)}), bf16[16,512,256]{2,1,0:T(8,128)(2,1)}, u32[]{:S(2)}, u32[]{:S(2)}) async-start(bf16[16,512,256]{2,1,0:T(8,128)(2,1)} %all-gather.2.cloned.1.call-done), calls=%async_computation | async-start | bytes 8388608 | tf_op jit(solution)/shard_map/all_to_all | solution.py:57
  96.8 0.0 copy-done.1
  96.8 63.2 %all_gather.9 = bf16[1,4,4,8192]{3,2,1,0:T(4,128)(2,1)S(1)} all-gather(bf16[1,4,4,1024]{3,2,1,0:T(4,128)(2,1)S(1)} %copy-done.1), channel_id=1, replica_groups=mesh['group'=16,'section'=2,'tensor'=8] {'tensor'}, dimensions={3}, use_global_device_ids=true | all-gather | bytes 294912 | tf_op jit(solution)/shard_map/all_gather | solution.py:49
  160.0 0.1 reshape.272
  160.1 0.0 copy-done.2
  160.1 0.0 copy-done.3
  160.2 0.1 add_convert_fusion
  160.2 0.1 iota_compare_fusion
  160.3 3.7 %select_reduce_fusion = (f32[4,4,8]{2,1,0:T(4,128)S(1)}, f32[4,4,8,4096]{3,2,1,0:T(8,128)S(1)}) fusion(pred[4,4096]{1,0:T(4,128)(4,1)S(1)} %iota_compare_fusion, bf16[4,4,8,128]{3,2,1,0:T(8,128)(2,1)S(1)} %reshape.276, bf16[1,4,1,4096,128]{4,3,2,1,0:T(8,128)(2,1)} %param.13), kind=kOutput, calls=%fused_computation.13 | convolution fusion | flops 135790464 | bytes 6341120 | tf_op jit(solution)/shard_map/rtjgh,rjph->rjtgp/dot_general | solution.py:79
  164.1 0.1 reshape.283
  164.2 0.2 copy.36
  164.3 3.0 %copy.26 = f32[1,16,16,32,2]{4,3,2,1,0:T(8,128)} copy(f32[1,16,16,32,2]{3,2,1,4,0:T(8,128)S(1)} %bitcast.90) | data formatting | bytes 131072 | tf_op jit(solution)/shard_map/convert_element_type | solution.py:29
  167.3 0.0 all-to-all-done
  167.3 6.5 %copy_bitcast_fusion = f32[1,16,16,32,256]{4,3,2,1,0:T(8,128)} fusion(bf16[1,16,16,32,256]{4,3,2,1,0:T(8,128)(2,1)} %bitcast.24), kind=kLoop, calls=%fused_computation | loop fusion | flops 2097152 | bytes 12582912 | tf_op jit(solution)/shard_map/convert_element_type | solution.py:30
  173.8 10.8 %reshape.280 = f32[8192,2,128]{2,1,0:T(2,128)} reshape(f32[1,16,16,32,256]{4,3,2,1,0:T(8,128)} %copy_bitcast_fusion) | data formatting | bytes 16777216 | tf_op jit(solution)/shard_map/convert_element_type | solution.py:30
  184.6 16.6 %multiply_convert_fusion = bf16[8192,2,128]{2,1,0:T(2,128)(2,1)S(1)} fusion(f32[8192,2,128]{2,1,0:T(2,128)} %reshape.280, f32[8192,2]{1,0:T(8,128)} %bitcast.88), kind=kLoop, calls=%fused_computation.1 | loop fusion | flops 4194304 | bytes 12648448 | tf_op jit(solution)/shard_map/convert_element_type | solution.py:30
  201.2 0.0 copy-start
  201.2 0.7 fusion.25
  201.9 1.5 copy-done
  203.4 0.7 fusion.22
  204.1 0.1 fusion.43
  204.2 0.3 select_reduce_fusion.1
  204.5 0.1 fusion.32
  204.6 0.6 fusion.8
  205.2 0.3 fusion.33
  205.5 3.0 %fusion.18 = bf16[4,4,1,8,128]{4,3,1,0,2:T(8,128)(2,1)S(1)} fusion(f32[4,128,4,8]{1,3,2,0:T(8,128)S(1)} %fusion.33, bf16[1,4,1,4096,128]{4,3,2,1,0:T(8,128)(2,1)} %param.14, f32[4,4,8,4096]{3,2,1,0:T(8,128)S(1)} %get-tuple-element.5, f32[4,4,8]{2,1,0:T(4,128)S(1)} %add.48, f32[4,4,8]{2,1,0:T(4,128)S(1)} %max.9, pred[4,4096]{1,0:T(4,128)(4,1)S(1)} %iota_compare_fusion), kind=kOutput, calls=%fused_computation.18 | convolution fusion | flops 136347648 | bytes 6407168 | tf_op jit(solution)/shard_map/rjtgp,rjph->rtjgh/dot_general | solution.py:101
  208.5 0.6 convert_element_type.118
  209.2 0.7 maximum_bitcast_fusion
  (7 shorter events, 0.1 us)
Async XLA Ops:
  7.2 84.4 %all-gather.2.cloned.1.call-start = ((), (), s32[]{:S(2)}) async-start(), calls=%async_computation.2 | async-start | bytes 4456448 | tf_op jit(solution)/shard_map/all_gather | solution.py:53
  68.8 28.0 %copy-start.1 = (bf16[1,4,4,1024]{3,2,1,0:T(4,128)(2,1)S(1)}, bf16[1,4,4,1024]{3,2,1,0:T(4,128)(2,1)}, u32[]{:S(2)}) copy-start(bf16[1,4,4,1024]{3,2,1,0:T(4,128)(2,1)} %param.8) | copy-start | bytes 98308
  68.8 91.3 %copy-start.2 = (bf16[1,4,4,1024]{3,2,1,0:T(4,128)(2,1)S(1)}, bf16[1,4,4,1024]{3,2,1,0:T(4,128)(2,1)}, u32[]{:S(2)}) copy-start(bf16[1,4,4,1024]{3,2,1,0:T(4,128)(2,1)} %param.12) | copy-start | bytes 98308
  68.8 91.3 %copy-start.3 = (s32[4]{0:T(128)S(1)}, s32[4]{0:T(128)}, u32[]{:S(2)}) copy-start(s32[4]{0:T(128)} %param.15) | copy-start | bytes 52
  91.5 75.8 %all-to-all-start = ((bf16[16,512,256]{2,1,0:T(8,128)(2,1)}), bf16[16,512,256]{2,1,0:T(8,128)(2,1)}, u32[]{:S(2)}, u32[]{:S(2)}) async-start(bf16[16,512,256]{2,1,0:T(8,128)(2,1)} %all-gather.2.cloned.1.call-done), calls=%async_computation | async-start | bytes 8388608 | tf_op jit(solution)/shard_map/all_to_all | solution.py:57
  201.2 2.2 %copy-start = (bf16[1,8192,256]{2,1,0:T(8,128)(2,1)S(1)}, bf16[1,8192,256]{2,1,0:T(8,128)(2,1)}, u32[]{:S(2)}) copy-start(bf16[1,8192,256]{2,1,0:T(8,128)(2,1)} %param.9) | copy-start | bytes 12582916
Sparse Core Ops, SparseCore 0:
  10.4 81.0 all-gather.1
where the time goes:
time: 217 us
  blocking collectives  123 us (57%)
  other arithmetic  24.8 us (11%)
  waiting for transfers between devices  23.4 us (11%)
  local copies, waits for them, and re-layouts  17.2 us (8%)
  between operations  14.2 us (7%)
  matrix products  8.67 us (4%)
  starting transfers between devices  5.28 us (2%)
    all_gather x1, blocking collectives, body(): features = lax.all_gather(hidden, 'tensor', axis=3, tiled=True)  63.2 us
    all_gather x1, blocking collectives, body(): lax.all_gather(delta_scales, 'group', axis=1, tiled=True)  42.5 us
    convert_element_type x2, other arithmetic, dequantize(): return (code_part.astype(jnp.float32) * scale_full).astype(jnp.bfloat16)  23.1 us
    all_gather x1, waiting for transfers between devices, body(): lax.all_gather(delta_codes, 'group', axis=1, tiled=True)  22.7 us
    all_to_all x1, blocking collectives, body(): lax.all_to_all(scales_all, ('section', 'tensor'), split_axis=0, concat_ax...  17.5 us
    convert_element_type x1, local copies, waits for them, and re-layouts, dequantize(): return (code_part.astype(jnp.float32) * scale_full).astype(jnp.bfloat16)  10.8 us
    all_to_all x1, starting transfers between devices, body(): lax.all_to_all(codes_all, ('section', 'tensor'), split_axis=0, concat_axi...  5.24 us
  transfers between devices with their start and end apart: 2, of which 1 were waited for; matrix products, arithmetic and copies ran while one was open for 4% of the time, Pallas kernels for 0%

commit v1 on v0

v1 whole, which is shorter than its diff:
```python
import functools
import math

import jax
import jax.numpy as jnp
from jax import lax
from jax.experimental import pallas as pl
from jax.experimental.pallas import tpu as pltpu
from jax.sharding import PartitionSpec as P

MESH = pl.DeviceIdType.MESH
LOG2E = math.log2(math.e)
TURN = 4


def place(g, s, t):
    return {"group": g, "section": s, "tensor": t}


def kernel(
    hidden, base, codes, scales, queries, keys, values, lengths,
    entries, attended,
    hidden_v, queries_v, codes_v, scales_v, base_v, keys_v, values_v,
    delta_out, delta_in, half_out, hidden_in, part_out, part_in,
    score_v, best_v, norm_v, mix_v, entries_v, attended_v,
    load_sem, cache_sem, delta_send, delta_recv, half_send, half_recv, spread_send, spread_recv,
    part_send, part_recv, store_sem,
):
    groups, sections, tensors = 16, 2, 8
    blocks = sections * tensors
    g = lax.axis_index("group")
    s = lax.axis_index("section")
    t = lax.axis_index("tensor")
    me = s * tensors + t
    rows, steps = hidden_v.shape[0], hidden_v.shape[1]
    tokens = rows * steps
    owned = codes_v.shape[1]
    chunk = blocks * owned
    heads = queries_v.shape[2] // 128
    asks = heads * steps
    context = keys_v.shape[1]

    loads = [
        pltpu.make_async_copy(codes, codes_v, load_sem.at[0]),
        pltpu.make_async_copy(scales, scales_v, load_sem.at[1]),
        pltpu.make_async_copy(hidden.at[0], hidden_v, load_sem.at[2]),
        pltpu.make_async_copy(queries.at[0], queries_v, load_sem.at[3]),
        pltpu.make_async_copy(base.at[0, pl.ds(g * chunk, chunk), :], base_v, load_sem.at[4]),
    ]
    caches = []
    for r in range(rows):
        caches.append(
            (
                pltpu.make_async_copy(keys.at[0, r, 0], keys_v.at[r], cache_sem.at[0, r]),
                pltpu.make_async_copy(values.at[0, r, 0], values_v.at[r], cache_sem.at[1, r]),
            )
        )
    for load in loads[:4]:
        load.start()

    inside = []
    for j in range(1, blocks):
        other = lax.rem(me + j, blocks)
        inside.append((other, lax.div(other, tensors), lax.rem(other, tensors)))
    across = [lax.rem(g + j, groups) for j in range(1, groups)]
    pair = lax.rem(t + tensors - TURN, tensors)
    half_to = [(2 * t + h, lax.rem(lax.div(g, 2) + TURN, tensors)) for h in range(2)]
    half_from = [(2 * pair + h, lax.div(g, 2)) for h in range(2)]

    barrier = pltpu.get_barrier_semaphore()
    for _, os, ot in inside:
        pl.semaphore_signal(barrier, inc=1, device_id=place(g, os, ot), device_id_type=MESH)
    for og, ot in half_to + half_from:
        pl.semaphore_signal(barrier, inc=1, device_id=place(og, s, ot), device_id_type=MESH)
    for og in across:
        pl.semaphore_signal(barrier, inc=1, device_id=place(og, s, t), device_id_type=MESH)

    for r in range(rows):
        for load in caches[r]:
            load.start()
    loads[4].start()

    loads[2].wait()
    slab = jnp.concatenate([hidden_v[r].astype(jnp.float32) for r in range(rows)], axis=0)
    for h in range(2):
        half_out[h] = slab[:, h * chunk : (h + 1) * chunk].astype(jnp.bfloat16)

    loads[0].wait()
    loads[1].wait()
    flat = scales_v[...].astype(jnp.float32).reshape(blocks * 2, owned)
    turned = flat.T
    for b in range(blocks):
        code = codes_v[b].astype(jnp.float32)
        left = code[:, :128] * turned[:, 2 * b : 2 * b + 1]
        right = code[:, 128:] * turned[:, 2 * b + 1 : 2 * b + 2]
        delta_out[b] = jnp.concatenate([left, right], axis=1).astype(jnp.bfloat16)

    pl.semaphore_wait(barrier, len(inside) + len(half_to) + len(half_from) + len(across))

    half_copies = []
    for h in range(2):
        og, ot = half_to[h]
        half_copies.append(
            pltpu.make_async_remote_copy(
                src_ref=half_out.at[h],
                dst_ref=hidden_in.at[g],
                send_sem=half_send,
                recv_sem=half_recv,
                device_id=place(og, s, ot),
                device_id_type=MESH,
            )
        )
        half_copies[-1].start()
    for other, os, ot in inside:
        pltpu.make_async_remote_copy(
            src_ref=delta_out.at[other],
            dst_ref=delta_in.at[me],
            send_sem=delta_send,
            recv_sem=delta_recv,
            device_id=place(g, os, ot),
            device_id_type=MESH,
        ).start()
    pltpu.make_async_copy(delta_out.at[me], delta_in.at[me], delta_recv).start()

    loads[3].wait()
    asked = []
    for r in range(rows):
        block = queries_v[r].astype(jnp.float32)
        asked.append(
            jnp.concatenate([block[:, h * 128 : (h + 1) * 128] for h in range(heads)], axis=0).astype(jnp.bfloat16)
        )
    scale = 128 ** -0.5 * LOG2E

    def attend(r):
        caches[r][0].wait()
        score = lax.dot_general(
            asked[r], keys_v[r], (((1,), (1,)), ((), ())), preferred_element_type=jnp.float32
        ) * scale
        place_of = lax.broadcasted_iota(jnp.int32, (asks, context), 1)
        score = jnp.where(place_of < lengths[r], score, -jnp.inf)
        best = jnp.max(score, axis=1, keepdims=True)
        weight = jnp.exp2(score - best)
        norm = jnp.sum(weight, axis=1, keepdims=True)
        caches[r][1].wait()
        mix = jnp.dot(weight.astype(jnp.bfloat16), values_v[r], preferred_element_type=jnp.float32)
        best_v[pl.ds(r * asks, asks), :] = jnp.broadcast_to(best, (asks, 128))
        norm_v[pl.ds(r * asks, asks), :] = jnp.broadcast_to(norm, (asks, 128))
        mix_v[pl.ds(r * asks, asks), :] = mix

    attend(0)

    mine = hidden_in.at[pl.ds(2 * pair, 2)]
    pltpu.make_async_copy(mine, mine, half_recv).wait()
    for j in range(1, tensors):
        pltpu.make_async_remote_copy(
            src_ref=mine,
            dst_ref=mine,
            send_sem=spread_send,
            recv_sem=spread_recv,
            device_id=place(g, s, lax.rem(t + j, tensors)),
            device_id_type=MESH,
        ).start()

    attend(1)
    attend(2)
    attend(3)

    loads[4].wait()
    pltpu.make_async_copy(delta_in, delta_in, delta_recv).wait()
    most = hidden_in.at[pl.ds(0, 2 * (tensors - 1))]
    pltpu.make_async_copy(most, most, spread_recv).wait()
    features = hidden_in[...].reshape(groups * tokens, chunk)
    update = delta_in[...].reshape(chunk, 256)
    partial = jnp.dot(features, base_v[...], preferred_element_type=jnp.float32)
    partial = partial + jnp.dot(features, update, preferred_element_type=jnp.float32)
    part_out[...] = partial.reshape(groups, tokens, 256).astype(jnp.bfloat16)
    for og in across:
        pltpu.make_async_remote_copy(
            src_ref=part_out.at[og],
            dst_ref=part_in.at[g],
            send_sem=part_send,
            recv_sem=part_recv,
            device_id=place(og, s, t),
            device_id_type=MESH,
        ).start()
    pltpu.make_async_copy(part_out.at[g], part_in.at[g], part_recv).start()

    line = lax.broadcasted_iota(jnp.int32, (tokens, 128), 0)
    lane = lax.broadcasted_iota(jnp.int32, (tokens, 128), 1)
    start = jnp.zeros((tokens, 128), jnp.int32)
    for r in range(rows):
        start = jnp.where(line // steps == r, lengths[r], start)
    position = (start + line % steps).astype(jnp.float32)
    frequency = jnp.exp((lane % 64).astype(jnp.float32) * (-2.0 * math.log(1000000.0) / 128))
    phase = position * frequency
    cosine = jnp.cos(phase)
    sine = jnp.where(lane < 64, -jnp.sin(phase), jnp.sin(phase))

    pltpu.make_async_copy(part_in, part_in, part_recv).wait()
    projected = jnp.sum(part_in[...].astype(jnp.float32), axis=0)
    key = projected[:, :128]
    swapped = jnp.concatenate([key[:, 64:], key[:, :64]], axis=1)
    fresh_key = key * cosine + swapped * sine
    fresh_value = projected[:, 128:]
    for r in range(rows):
        lines = slice(r * steps, (r + 1) * steps)
        entries_v[r] = jnp.concatenate([fresh_key[lines], fresh_value[lines]], axis=1).astype(jnp.bfloat16)
    store_entries = pltpu.make_async_copy(entries_v, entries.at[0], store_sem.at[0])
    store_entries.start()

    every = jnp.concatenate(asked, axis=0)
    total = rows * asks
    score = lax.dot_general(
        every, fresh_key.astype(jnp.bfloat16), (((1,), (1,)), ((), ())), preferred_element_type=jnp.float32
    ) * scale
    line = lax.broadcasted_iota(jnp.int32, (total, tokens), 0)
    col = lax.broadcasted_iota(jnp.int32, (total, tokens), 1)
    seen = (line // asks == col // steps) & (col % steps <= line % steps)
    score = jnp.where(seen, score, -jnp.inf)
    best_old = best_v[:, :1]
    best = jnp.maximum(best_old, jnp.max(score, axis=1, keepdims=True))
    weight = jnp.exp2(score - best)
    decay = jnp.exp2(best_old - best)
    norm = norm_v[:, :1] * decay + jnp.sum(weight, axis=1, keepdims=True)
    mix = mix_v[...] * decay + jnp.dot(
        weight.astype(jnp.bfloat16), fresh_value.astype(jnp.bfloat16), preferred_element_type=jnp.float32
    )
    result = mix / norm
    for r in range(rows):
        for h in range(heads):
            at = r * asks + h * steps
            attended_v[r, :, h * 128 : (h + 1) * 128] = result[at : at + steps].astype(jnp.bfloat16)
    store_attended = pltpu.make_async_copy(attended_v, attended.at[0], store_sem.at[1])
    store_attended.start()

    for copy in half_copies:
        copy.wait_send()
    sent = delta_out.at[pl.ds(0, blocks - 1)]
    pltpu.make_async_copy(sent, sent, delta_send).wait()
    pltpu.make_async_copy(most, most, spread_send).wait()
    sent = part_out.at[pl.ds(0, groups - 1)]
    pltpu.make_async_copy(sent, sent, part_send).wait()
    store_entries.wait()
    store_attended.wait()


def body(hidden, base_kv, delta_codes, delta_scales, queries, key_cache, value_cache, lengths):
    rows, steps, slab = hidden.shape[1:]
    blocks, owned, width = delta_codes.shape
    chunk = blocks * owned
    context = key_cache.shape[3]
    groups = lax.axis_size("group")
    tokens = rows * steps
    asks = rows * queries.shape[3] // 128 * steps
    any_space = pl.BlockSpec(memory_space=pl.ANY)
    bf16, f32 = jnp.bfloat16, jnp.float32
    return pl.pallas_call(
        kernel,
        out_shape=(
            jax.ShapeDtypeStruct((1, rows, steps, width), bf16),
            jax.ShapeDtypeStruct((1, rows, steps, queries.shape[3]), bf16),
        ),
        in_specs=[any_space] * 7 + [pl.BlockSpec(memory_space=pltpu.SMEM)],
        out_specs=[any_space, any_space],
        scratch_shapes=[
            pltpu.VMEM((rows, steps, slab), bf16),
            pltpu.VMEM((rows, steps, queries.shape[3]), bf16),
            pltpu.VMEM((blocks, owned, width), bf16),
            pltpu.VMEM((blocks, 2, owned), bf16),
            pltpu.VMEM((chunk, width), bf16),
            pltpu.VMEM((rows, context, 128), bf16),
            pltpu.VMEM((rows, context, 128), bf16),
            pltpu.VMEM((blocks, owned, width), bf16),
            pltpu.VMEM((blocks, owned, width), bf16),
            pltpu.VMEM((2, tokens, chunk), bf16),
            pltpu.VMEM((groups, tokens, chunk), bf16),
            pltpu.VMEM((groups, tokens, width), bf16),
            pltpu.VMEM((groups, tokens, width), bf16),
            pltpu.VMEM((8, 128), f32),
            pltpu.VMEM((asks, 128), f32),
            pltpu.VMEM((asks, 128), f32),
            pltpu.VMEM((asks, 128), f32),
            pltpu.VMEM((rows, steps, width), bf16),
            pltpu.VMEM((rows, steps, queries.shape[3]), bf16),
            pltpu.SemaphoreType.DMA((5,)),
            pltpu.SemaphoreType.DMA((2, rows)),
            pltpu.SemaphoreType.DMA,
            pltpu.SemaphoreType.DMA,
            pltpu.SemaphoreType.DMA,
            pltpu.SemaphoreType.DMA,
            pltpu.SemaphoreType.DMA,
            pltpu.SemaphoreType.DMA,
            pltpu.SemaphoreType.DMA,
            pltpu.SemaphoreType.DMA,
            pltpu.SemaphoreType.DMA((2,)),
        ],
        compiler_params=pltpu.CompilerParams(
            collective_id=0, has_side_effects=True, vmem_limit_bytes=62 * 1024 * 1024
        ),
    )(
        hidden, base_kv, delta_codes, jnp.transpose(delta_scales, (0, 2, 1)),
        queries, key_cache, value_cache, lengths,
    )


def solution(mesh):
    placed = (
        P("section", "group", None, "tensor"),
        P(("section", "tensor"), None, None),
        P(None, ("group", "section", "tensor"), None),
        P(None, ("group", "section", "tensor"), None),
        P("section", "group", None, "tensor"),
        P("section", "group", "tensor", None, None),
        P("section", "group", "tensor", None, None),
        P("group"),
    )
    return jax.shard_map(
        body,
        mesh=mesh,
        in_specs=placed,
        out_specs=(P("section", "group", None, "tensor"), P("section", "group", None, "tensor")),
        check_vma=False,
    )
```

time: 217 us -> 35.3 us (0.16)
  the two profiles are of different devices: /device:TPU:7 before, /device:TPU:1 now
where the time goes in v1:
time: 35.3 us; the launch traced here: 35.1 us
  Pallas kernels  31.7 us (90%)
  local copies, waits for them, and re-layouts  2.68 us (8%)
  between operations  0.64 us (2%)
    pallas_call x1, Pallas kernels, body(): pl.pallas_call(kernel, out_shape=(jax.ShapeDtypeStruct((1, rows, steps, w...  31.7 us
    unnamed x2, local copies, waits for them, and re-layouts  2.68 us

profile of v1, /device:TPU:1, one launch (start us, length us, event | category | flops | bytes accessed | tf_op | source)
XLA Modules:
  0.0 35.1 jit_solution(8805649463101869049)
XLA Ops:
  0.6 31.7 %shard_map.95 = (bf16[1,4,4,256]{3,2,1,0:T(4,128)(2,1)}, bf16[1,4,4,1024]{3,2,1,0:T(4,128)(2,1)}) custom-call(bf16[1,4,4,1024]{3,2,1,0:T(4,128)(2,1)} %hidden.1, bf16[1,8192,256]{2,1,0:T(8,128)(2,1)} %base.1, bf16[16,32,256]{2,1,0:T(8,128)(2,1)} %codes.1, bf16[16,2,32]{2,1,0:T(2,128)(2,1)} %bitcast.1, bf16[1,4,4,1024]{3,2,1,0:T(4,128)(2,1)} %queries.1, ...), custom_call_target="tpu_custom_call" | custom-call | tf_op jit(solution)/shard_map/pallas_call | solution.py:257
  32.4 1.3 %copy.12 = bf16[1,4,4,256]{3,2,1,0:T(4,128)(2,1)} copy(bf16[1,4,4,256]{3,2,1,0:T(4,128)(2,1)} %get-tuple-element.4) | data formatting | bytes 16384
  33.7 1.4 %copy.13 = bf16[1,4,4,1024]{3,2,1,0:T(4,128)(2,1)} copy(bf16[1,4,4,1024]{3,2,1,0:T(4,128)(2,1)} %get-tuple-element.5) | data formatting | bytes 65536

commit v2 on v1

v2 whole, which is shorter than its diff:
```python
import math

import jax
import jax.numpy as jnp
from jax import lax
from jax.experimental import pallas as pl
from jax.experimental.pallas import tpu as pltpu
from jax.sharding import PartitionSpec as P

MESH = pl.DeviceIdType.MESH
LOG2E = math.log2(math.e)
SCALE = 128 ** -0.5 * LOG2E
HIGH, WIDE, TENSORS, SECTIONS = 4, 4, 8, 2
GROUPS = HIGH * WIDE
BLOCKS = SECTIONS * TENSORS
HALF = GROUPS // 2


def exchange(
    hidden, base, codes, scales, queries, keys, values, lengths,
    projected, asked, best, norm, mix,
    hidden_v, queries_v, codes_v, scales_v, base_v, keys_v, values_v,
    delta_out, delta_in, half_out, hidden_in, part_out, part_in,
    load_sem, cache_sem, delta_send, delta_recv, pass_send, pass_recv, base_send, base_recv,
    half_send, half_recv, part_send, part_recv,
):
    g = lax.axis_index("group")
    s = lax.axis_index("section")
    t = lax.axis_index("tensor")
    me = s * TENSORS + t
    chip = lax.div(t, 2)
    core = lax.rem(t, 2)
    high = lax.div(g, WIDE)
    wide = lax.rem(g, WIDE)
    rows, steps = hidden_v.shape[0], hidden_v.shape[1]
    owned = codes_v.shape[1]
    chunk = BLOCKS * owned
    heads = queries_v.shape[2] // 128
    asks = heads * steps
    context = keys_v.shape[1]

    def at(og, os, ot):
        return {"group": og, "section": os, "tensor": ot}

    side = 1 - lax.div(wide, 2)
    first = 2 * (1 - core)
    sibling = 2 * chip + 1 - core
    inside = []
    for j in range(1, BLOCKS):
        other = lax.rem(me + j, BLOCKS)
        inside.append((other, at(g, lax.div(other, TENSORS), lax.rem(other, TENSORS))))
    turns = (2, 1, 3, 0)
    taken = []
    for i in turns:
        for j in range(2):
            oh = lax.rem(high + i, HIGH)
            taken.append((i, j, oh * 2 + j, oh * WIDE + first + j))

    barrier = pltpu.get_barrier_semaphore()
    for _, _, _, og in taken:
        pl.semaphore_signal(barrier, inc=1, device_id=at(og, s, lax.div(g, 2)), device_id_type=MESH)
    for j in range(1, GROUPS):
        og = lax.rem(g + j, GROUPS)
        pl.semaphore_signal(barrier, inc=1, device_id=at(og, s, 2 * chip + side), device_id_type=MESH)
    for _, there in inside:
        pl.semaphore_signal(barrier, inc=1, device_id=there, device_id_type=MESH)

    loads = [
        pltpu.make_async_copy(hidden.at[0], hidden_v, load_sem.at[0]),
        pltpu.make_async_copy(codes, codes_v, load_sem.at[1]),
        pltpu.make_async_copy(scales, scales_v, load_sem.at[2]),
        pltpu.make_async_copy(queries.at[0], queries_v, load_sem.at[3]),
        pltpu.make_async_copy(base.at[0, pl.ds(g * chunk, chunk), :], base_v.at[core], load_sem.at[4]),
    ]
    for load in loads:
        load.start()
    caches = []
    for r in range(rows):
        caches.append(
            (
                pltpu.make_async_copy(keys.at[0, r, 0], keys_v.at[r], cache_sem.at[0, r]),
                pltpu.make_async_copy(values.at[0, r, 0], values_v.at[r], cache_sem.at[1, r]),
            )
        )
        for load in caches[r]:
            load.start()

    loads[0].wait()
    slab = jnp.concatenate([hidden_v[r].astype(jnp.float32) for r in range(rows)], axis=0)
    for h in range(2):
        half_out[h] = slab[:, h * chunk : (h + 1) * chunk].astype(jnp.bfloat16)

    own = (side == core).astype(jnp.int32)
    pl.semaphore_wait(barrier, len(inside) + 2 * WIDE + 2 * HALF - 2 * own)

    half_copies = []
    for h in range(2):
        for i in turns:
            half_copies.append(
                pltpu.make_async_remote_copy(
                    src_ref=half_out.at[h],
                    dst_ref=hidden_in.at[high * 2 + lax.rem(wide, 2)],
                    send_sem=half_send,
                    recv_sem=half_recv,
                    device_id=at(2 * t + h, s, 2 * lax.rem(chip + i, 4) + side),
                    device_id_type=MESH,
                )
            )
            half_copies[-1].start()

    loads[1].wait()
    loads[2].wait()
    turned = scales_v[...].astype(jnp.float32).reshape(BLOCKS * 2, owned).T
    for b in range(BLOCKS):
        code = codes_v[b].astype(jnp.float32)
        left = code[:, :128] * turned[:, 2 * b : 2 * b + 1]
        right = code[:, 128:] * turned[:, 2 * b + 1 : 2 * b + 2]
        delta_out[b] = jnp.concatenate([left, right], axis=1).astype(jnp.bfloat16)
    for other, there in inside:
        pltpu.make_async_remote_copy(
            src_ref=delta_out.at[other],
            dst_ref=delta_in.at[lax.rem(other, 2), me],
            send_sem=delta_send,
            recv_sem=delta_recv,
            device_id=there,
            device_id_type=MESH,
        ).start()
    pltpu.make_async_copy(delta_out.at[me], delta_in.at[core, me], delta_recv).start()

    loads[4].wait()
    base_copy = pltpu.make_async_remote_copy(
        src_ref=base_v.at[core],
        dst_ref=base_v.at[core],
        send_sem=base_send,
        recv_sem=base_recv,
        device_id=at(g, s, sibling),
        device_id_type=MESH,
    )
    base_copy.start()

    loads[3].wait()
    for r in range(rows):
        block = queries_v[r].astype(jnp.float32)
        asked[pl.ds(r * asks, asks), :] = jnp.concatenate(
            [block[:, h * 128 : (h + 1) * 128] for h in range(heads)], axis=0
        ).astype(jnp.bfloat16)

    def attend(r):
        lines = pl.ds(r * asks, asks)
        caches[r][0].wait()
        score = lax.dot_general(
            asked[lines, :], keys_v[r], (((1,), (1,)), ((), ())), preferred_element_type=jnp.float32
        ) * SCALE
        place = lax.broadcasted_iota(jnp.int32, (asks, context), 1)
        score = jnp.where(place < lengths[r], score, -jnp.inf)
        peak = jnp.max(score, axis=1, keepdims=True)
        weight = jnp.exp2(score - peak)
        total = jnp.sum(weight, axis=1, keepdims=True)
        caches[r][1].wait()
        best[lines, :] = jnp.broadcast_to(peak, (asks, 128))
        norm[lines, :] = jnp.broadcast_to(total, (asks, 128))
        mix[lines, :] = jnp.dot(weight.astype(jnp.bfloat16), values_v[r], preferred_element_type=jnp.float32)

    attend(0)
    attend(1)

    mine = delta_in.at[core]
    pltpu.make_async_copy(mine, mine, delta_recv).wait()
    pass_copy = pltpu.make_async_remote_copy(
        src_ref=mine,
        dst_ref=mine,
        send_sem=pass_send,
        recv_sem=pass_recv,
        device_id=at(g, s, sibling),
        device_id_type=MESH,
    )
    pass_copy.start()

    attend(2)
    attend(3)

    base_copy.wait_recv()
    pass_copy.wait_recv()
    pltpu.make_async_copy(hidden_in, hidden_in, half_recv).wait()
    features = hidden_in[...].reshape(HALF * rows * steps, chunk)
    for c in range(2):
        part = jnp.dot(features, base_v[c], preferred_element_type=jnp.float32)
        part = part + jnp.dot(
            features, delta_in[c].reshape(chunk, part.shape[1]), preferred_element_type=jnp.float32
        )
        part_out[c] = part.reshape(HALF, rows * steps, part.shape[1]).astype(jnp.bfloat16)

    def send_part(c, slot, og):
        return pltpu.make_async_remote_copy(
            src_ref=part_out.at[c, slot],
            dst_ref=part_in.at[g],
            send_sem=part_send,
            recv_sem=part_recv,
            device_id=at(og, s, 2 * chip + c),
            device_id_type=MESH,
        )

    for i, j, slot, og in taken:
        for c in range(2):
            if i == 0:
                local = (og == g) & (core == c)

                @pl.when(local)
                def _():
                    pltpu.make_async_copy(part_out.at[c, slot], part_in.at[g], part_recv).start()

                @pl.when(jnp.logical_not(local))
                def _():
                    send_part(c, slot, og).start()
            else:
                send_part(c, slot, og).start()

    pltpu.make_async_copy(part_in, part_in, part_recv).wait()
    projected[...] = jnp.sum(part_in[...].astype(jnp.float32), axis=0)

    for copy in half_copies:
        copy.wait_send()
    sent = delta_out.at[pl.ds(0, BLOCKS - 1)]
    pltpu.make_async_copy(sent, sent, delta_send).wait()
    base_copy.wait_send()
    pass_copy.wait_send()
    for i, j, slot, og in taken:
        for c in range(2):
            if i == 0:

                @pl.when(jnp.logical_not((og == g) & (core == c)))
                def _():
                    send_part(c, slot, og).wait_send()
            else:
                send_part(c, slot, og).wait_send()


def finish(lengths, projected, asked, best, norm, mix, entries, attended, entries_v, attended_v, store_sem):
    rows, steps = entries_v.shape[0], entries_v.shape[1]
    tokens = rows * steps
    total = asked.shape[0]
    asks = total // rows
    heads = asks // steps

    line = lax.broadcasted_iota(jnp.int32, (tokens, 128), 0)
    lane = lax.broadcasted_iota(jnp.int32, (tokens, 128), 1)
    start = jnp.zeros((tokens, 128), jnp.int32)
    for r in range(rows):
        start = jnp.where(line // steps == r, lengths[r], start)
    position = (start + line % steps).astype(jnp.float32)
    frequency = jnp.exp((lane % 64).astype(jnp.float32) * (-2.0 * math.log(1000000.0) / 128))
    phase = position * frequency
    cosine = jnp.cos(phase)
    sine = jnp.where(lane < 64, -jnp.sin(phase), jnp.sin(phase))

    key = projected[:, :128]
    swapped = jnp.concatenate([key[:, 64:], key[:, :64]], axis=1)
    fresh_key = key * cosine + swapped * sine
    fresh_value = projected[:, 128:]
    for r in range(rows):
        lines = slice(r * steps, (r + 1) * steps)
        entries_v[r] = jnp.concatenate([fresh_key[lines], fresh_value[lines]], axis=1).astype(jnp.bfloat16)
    store_entries = pltpu.make_async_copy(entries_v, entries.at[0], store_sem.at[0])
    store_entries.start()

    score = lax.dot_general(
        asked[...], fresh_key.astype(jnp.bfloat16), (((1,), (1,)), ((), ())), preferred_element_type=jnp.float32
    ) * SCALE
    line = lax.broadcasted_iota(jnp.int32, (total, tokens), 0)
    col = lax.broadcasted_iota(jnp.int32, (total, tokens), 1)
    seen = (line // asks == col // steps) & (col % steps <= line % steps)
    score = jnp.where(seen, score, -jnp.inf)
    old = best[:, :1]
    peak = jnp.maximum(old, jnp.max(score, axis=1, keepdims=True))
    weight = jnp.exp2(score - peak)
    decay = jnp.exp2(old - peak)
    whole = norm[:, :1] * decay + jnp.sum(weight, axis=1, keepdims=True)
    result = mix[...] * decay + jnp.dot(
        weight.astype(jnp.bfloat16), fresh_value.astype(jnp.bfloat16), preferred_element_type=jnp.float32
    )
    result = result / whole
    for r in range(rows):
        for h in range(heads):
            at = r * asks + h * steps
            attended_v[r, :, h * 128 : (h + 1) * 128] = result[at : at + steps].astype(jnp.bfloat16)
    store_attended = pltpu.make_async_copy(attended_v, attended.at[0], store_sem.at[1])
    store_attended.start()
    store_entries.wait()
    store_attended.wait()


def body(hidden, base_kv, delta_codes, delta_scales, queries, key_cache, value_cache, lengths):
    rows, steps, slab = hidden.shape[1:]
    owned, width = delta_codes.shape[1:]
    chunk = BLOCKS * owned
    context = key_cache.shape[3]
    query_width = queries.shape[3]
    tokens = rows * steps
    asks = rows * query_width // 128 * steps
    anywhere = pl.BlockSpec(memory_space=pl.ANY)
    scalars = pl.BlockSpec(memory_space=pltpu.SMEM)
    fast = pl.BlockSpec(memory_space=pltpu.VMEM)
    bf16, f32 = jnp.bfloat16, jnp.float32
    dma = pltpu.SemaphoreType.DMA
    middle = pl.pallas_call(
        exchange,
        out_shape=(
            pltpu.VMEM((tokens, width), f32),
            pltpu.VMEM((asks, 128), bf16),
            pltpu.VMEM((asks, 128), f32),
            pltpu.VMEM((asks, 128), f32),
            pltpu.VMEM((asks, 128), f32),
        ),
        in_specs=[anywhere] * 7 + [scalars],
        out_specs=[fast] * 5,
        scratch_shapes=[
            pltpu.VMEM((rows, steps, slab), bf16),
            pltpu.VMEM((rows, steps, query_width), bf16),
            pltpu.VMEM((BLOCKS, owned, width), bf16),
            pltpu.VMEM((BLOCKS, 2, owned), bf16),
            pltpu.VMEM((2, chunk, width), bf16),
            pltpu.VMEM((rows, context, 128), bf16),
            pltpu.VMEM((rows, context, 128), bf16),
            pltpu.VMEM((BLOCKS, owned, width), bf16),
            pltpu.VMEM((2, BLOCKS, owned, width), bf16),
            pltpu.VMEM((2, tokens, chunk), bf16),
            pltpu.VMEM((HALF, tokens, chunk), bf16),
            pltpu.VMEM((2, HALF, tokens, width), bf16),
            pltpu.VMEM((GROUPS, tokens, width), bf16),
            dma((5,)),
            dma((2, rows)),
            dma, dma, dma, dma, dma, dma, dma, dma, dma, dma,
        ],
        compiler_params=pltpu.CompilerParams(
            collective_id=0, has_side_effects=True, vmem_limit_bytes=60 * 1024 * 1024
        ),
    )(
        hidden, base_kv, delta_codes, jnp.transpose(delta_scales, (0, 2, 1)),
        queries, key_cache, value_cache, lengths,
    )
    return pl.pallas_call(
        finish,
        out_shape=(
            jax.ShapeDtypeStruct((1, rows, steps, width), bf16),
            jax.ShapeDtypeStruct((1, rows, steps, query_width), bf16),
        ),
        in_specs=[scalars] + [fast] * 5,
        out_specs=[anywhere, anywhere],
        scratch_shapes=[
            pltpu.VMEM((rows, steps, width), bf16),
            pltpu.VMEM((rows, steps, query_width), bf16),
            dma((2,)),
        ],
        compiler_params=pltpu.CompilerParams(vmem_limit_bytes=8 * 1024 * 1024),
    )(lengths, *middle)


def solution(mesh):
    placed = (
        P("section", "group", None, "tensor"),
        P(("section", "tensor"), None, None),
        P(None, ("group", "section", "tensor"), None),
        P(None, ("group", "section", "tensor"), None),
        P("section", "group", None, "tensor"),
        P("section", "group", "tensor", None, None),
        P("section", "group", "tensor", None, None),
        P("group"),
    )
    return jax.shard_map(
        body,
        mesh=mesh,
        in_specs=placed,
        out_specs=(P("section", "group", None, "tensor"), P("section", "group", None, "tensor")),
        check_vma=False,
    )
```

time: 35.3 us -> 33.1 us (0.938)
  local copies, waits for them, and re-layouts: 2.68 us -> 0.01 us
  Pallas kernels: 31.7 us -> 32.4 us
    unnamed x2, local copies, waits for them, and re-layouts: 2.68 us -> 0.01 us
    pallas_call x1 -> x2, Pallas kernels: 31.7 us -> 32.4 us  [the longest x1 30.7 us: body(): pl.pallas_call(exchange, out_shape=(pltpu.VMEM((tokens, width), f32), plt...]
where the time goes in v2:
time: 33.1 us; the launch traced here: 33 us
  Pallas kernels  32.4 us (98%)
  between operations  0.66 us (2%)
    pallas_call x1, Pallas kernels, body(): pl.pallas_call(exchange, out_shape=(pltpu.VMEM((tokens, width), f32), plt...  30.7 us
    pallas_call x1, Pallas kernels, body(): pl.pallas_call(finish, out_shape=(jax.ShapeDtypeStruct((1, rows, steps, w...  1.7 us

profile of v2, /device:TPU:1, one launch (start us, length us, event | category | flops | bytes accessed | tf_op | source)
XLA Modules:
  0.0 33.0 jit_solution(8953764964294137966)
XLA Ops:
  0.6 0.0 copy-start
  0.6 30.7 %shard_map.95 = (f32[16,256]{1,0:T(8,128)S(1)}, bf16[128,128]{1,0:T(8,128)(2,1)S(1)}, f32[128,128]{1,0:T(8,128)S(1)}, f32[128,128]{1,0:T(8,128)S(1)}, f32[128,128]{1,0:T(8,128)S(1)}) custom-call(bf16[1,4,4,1024]{3,2,1,0:T(4,128)(2,1)} %hidden.1, bf16[1,8192,256]{2,1,0:T(8,128)(2,1)} %base.1, bf16[16,32,256]{2,1,0:T(8,128)(2,1)} %codes.1, ...), custom_call_target="tpu_custom_call" | custom-call | tf_op jit(solution)/shard_map/pallas_call | solution.py:305
  31.3 0.0 copy-done
  31.3 1.7 %shard_map.96 = (bf16[1,4,4,256]{3,2,1,0:T(4,128)(2,1)}, bf16[1,4,4,1024]{3,2,1,0:T(4,128)(2,1)}) custom-call(s32[4]{0:T(128)S(1)} %copy-done, f32[16,256]{1,0:T(8,128)S(1)} %get-tuple-element.7.projected, bf16[128,128]{1,0:T(8,128)(2,1)S(1)} %get-tuple-element.8.asked, f32[128,128]{1,0:T(8,128)S(1)} %get-tuple-element.9.best, ...), custom_call_target="tpu_custom_call" | custom-call | tf_op jit(solution)/shard_map/pallas_call | solution.py:341
Async XLA Ops:
  0.6 30.7 %copy-start = (s32[4]{0:T(128)S(1)}, s32[4]{0:T(128)}, u32[]{:S(2)}) copy-start(s32[4]{0:T(128)} %lengths.3) | copy-start | bytes 52

commit v3 on v2

--- a/solution.py
+++ b/solution.py
@@ -22,7 +22,7 @@
     hidden_v, queries_v, codes_v, scales_v, base_v, keys_v, values_v,
     delta_out, delta_in, half_out, hidden_in, part_out, part_in,
     load_sem, cache_sem, delta_send, delta_recv, pass_send, pass_recv, base_send, base_recv,
-    half_send, half_recv, part_send, part_recv,
+    half_send, half_recv, spread_send, spread_recv, part_send, part_recv,
 ):
     g = lax.axis_index("group")
     s = lax.axis_index("section")
@@ -42,26 +42,27 @@
     def at(og, os, ot):
         return {"group": og, "section": os, "tensor": ot}
 
-    side = 1 - lax.div(wide, 2)
-    first = 2 * (1 - core)
+    first = 2 * core
     sibling = 2 * chip + 1 - core
+    turns = (2, 1, 3, 0)
     inside = []
-    for j in range(1, BLOCKS):
-        other = lax.rem(me + j, BLOCKS)
-        inside.append((other, at(g, lax.div(other, TENSORS), lax.rem(other, TENSORS))))
-    turns = (2, 1, 3, 0)
+    for i in turns:
+        for ds in (1, 0):
+            for dc in (1, 0):
+                if i or ds or dc:
+                    os, ot = lax.rem(s + ds, 2), 2 * lax.rem(chip + i, 4) + lax.rem(core + dc, 2)
+                    inside.append((os * TENSORS + ot, at(g, os, ot)))
+    relay = lax.rem(t + TENSORS // 2, TENSORS)
+    relay_slot = 2 * lax.div(relay, 2)
     taken = []
     for i in turns:
-        for j in range(2):
+        for j in (1, 0):
             oh = lax.rem(high + i, HIGH)
             taken.append((i, j, oh * 2 + j, oh * WIDE + first + j))
 
     barrier = pltpu.get_barrier_semaphore()
-    for _, _, _, og in taken:
-        pl.semaphore_signal(barrier, inc=1, device_id=at(og, s, lax.div(g, 2)), device_id_type=MESH)
-    for j in range(1, GROUPS):
-        og = lax.rem(g + j, GROUPS)
-        pl.semaphore_signal(barrier, inc=1, device_id=at(og, s, 2 * chip + side), device_id_type=MESH)
+    for h in range(2):
+        pl.semaphore_signal(barrier, inc=1, device_id=at(2 * relay + h, s, lax.div(g, 2)), device_id_type=MESH)
     for _, there in inside:
         pl.semaphore_signal(barrier, inc=1, device_id=there, device_id_type=MESH)
 
@@ -90,24 +91,6 @@
     for h in range(2):
         half_out[h] = slab[:, h * chunk : (h + 1) * chunk].astype(jnp.bfloat16)
 
-    own = (side == core).astype(jnp.int32)
-    pl.semaphore_wait(barrier, len(inside) + 2 * WIDE + 2 * HALF - 2 * own)
-
-    half_copies = []
-    for h in range(2):
-        for i in turns:
-            half_copies.append(
-                pltpu.make_async_remote_copy(
-                    src_ref=half_out.at[h],
-                    dst_ref=hidden_in.at[high * 2 + lax.rem(wide, 2)],
-                    send_sem=half_send,
-                    recv_sem=half_recv,
-                    device_id=at(2 * t + h, s, 2 * lax.rem(chip + i, 4) + side),
-                    device_id_type=MESH,
-                )
-            )
-            half_copies[-1].start()
-
     loads[1].wait()
     loads[2].wait()
     turned = scales_v[...].astype(jnp.float32).reshape(BLOCKS * 2, owned).T
@@ -116,6 +99,22 @@
         left = code[:, :128] * turned[:, 2 * b : 2 * b + 1]
         right = code[:, 128:] * turned[:, 2 * b + 1 : 2 * b + 2]
         delta_out[b] = jnp.concatenate([left, right], axis=1).astype(jnp.bfloat16)
+
+    pl.semaphore_wait(barrier, len(inside) + 2)
+
+    half_copies = []
+    for h in range(2):
+        half_copies.append(
+            pltpu.make_async_remote_copy(
+                src_ref=half_out.at[h],
+                dst_ref=hidden_in.at[high * 2 + lax.rem(wide, 2)],
+                send_sem=half_send,
+                recv_sem=half_recv,
+                device_id=at(2 * t + h, s, lax.rem(lax.div(g, 2) + TENSORS // 2, TENSORS)),
+                device_id_type=MESH,
+            )
+        )
+        half_copies[-1].start()
     for other, there in inside:
         pltpu.make_async_remote_copy(
             src_ref=delta_out.at[other],
@@ -164,6 +163,22 @@
     attend(0)
     attend(1)
 
+    here = hidden_in.at[pl.ds(relay_slot, 2)]
+    pltpu.make_async_copy(here, here, half_recv).wait()
+    spread_copies = []
+    for i in turns[:3]:
+        spread_copies.append(
+            pltpu.make_async_remote_copy(
+                src_ref=here,
+                dst_ref=here,
+                send_sem=spread_send,
+                recv_sem=spread_recv,
+                device_id=at(g, s, 2 * lax.rem(chip + i, 4) + core),
+                device_id_type=MESH,
+            )
+        )
+        spread_copies[-1].start()
+
     mine = delta_in.at[core]
     pltpu.make_async_copy(mine, mine, delta_recv).wait()
     pass_copy = pltpu.make_async_remote_copy(
@@ -181,7 +196,8 @@
 
     base_copy.wait_recv()
     pass_copy.wait_recv()
-    pltpu.make_async_copy(hidden_in, hidden_in, half_recv).wait()
+    most = hidden_in.at[pl.ds(0, HALF - 2)]
+    pltpu.make_async_copy(most, most, spread_recv).wait()
     features = hidden_in[...].reshape(HALF * rows * steps, chunk)
     for c in range(2):
         part = jnp.dot(features, base_v[c], preferred_element_type=jnp.float32)
@@ -218,7 +234,7 @@
     pltpu.make_async_copy(part_in, part_in, part_recv).wait()
     projected[...] = jnp.sum(part_in[...].astype(jnp.float32), axis=0)
 
-    for copy in half_copies:
+    for copy in half_copies + spread_copies:
         copy.wait_send()
     sent = delta_out.at[pl.ds(0, BLOCKS - 1)]
     pltpu.make_async_copy(sent, sent, delta_send).wait()
@@ -329,7 +345,7 @@
             pltpu.VMEM((GROUPS, tokens, width), bf16),
             dma((5,)),
             dma((2, rows)),
-            dma, dma, dma, dma, dma, dma, dma, dma, dma, dma,
+            dma, dma, dma, dma, dma, dma, dma, dma, dma, dma, dma, dma,
         ],
         compiler_params=pltpu.CompilerParams(
             collective_id=0, has_side_effects=True, vmem_limit_bytes=60 * 1024 * 1024

time: 33.1 us -> 31.4 us (0.949)
  Pallas kernels: 32.4 us -> 30.6 us
    pallas_call x1, Pallas kernels: 30.7 us -> 28.9 us  [body(): pl.pallas_call(exchange, out_shape=(pltpu.VMEM((tokens, width), f32), plt...]
where the time goes in v3:
time: 31.4 us; the launch traced here: 31.3 us
  Pallas kernels  30.6 us (97%)
  between operations  0.66 us (2%)
    pallas_call x1, Pallas kernels, body(): pl.pallas_call(exchange, out_shape=(pltpu.VMEM((tokens, width), f32), plt...  28.9 us
    pallas_call x1, Pallas kernels, body(): pl.pallas_call(finish, out_shape=(jax.ShapeDtypeStruct((1, rows, steps, w...  1.7 us

profile of v3, /device:TPU:1, one launch (start us, length us, event | category | flops | bytes accessed | tf_op | source)
XLA Modules:
  0.0 31.3 jit_solution(18277477135840778965)
XLA Ops:
  0.6 0.0 copy-start
  0.6 28.9 %shard_map.95 = (f32[16,256]{1,0:T(8,128)S(1)}, bf16[128,128]{1,0:T(8,128)(2,1)S(1)}, f32[128,128]{1,0:T(8,128)S(1)}, f32[128,128]{1,0:T(8,128)S(1)}, f32[128,128]{1,0:T(8,128)S(1)}) custom-call(bf16[1,4,4,1024]{3,2,1,0:T(4,128)(2,1)} %hidden.1, bf16[1,8192,256]{2,1,0:T(8,128)(2,1)} %base.1, bf16[16,32,256]{2,1,0:T(8,128)(2,1)} %codes.1, ...), custom_call_target="tpu_custom_call" | custom-call | tf_op jit(solution)/shard_map/pallas_call | solution.py:321
  29.6 0.0 copy-done
  29.6 1.7 %shard_map.96 = (bf16[1,4,4,256]{3,2,1,0:T(4,128)(2,1)}, bf16[1,4,4,1024]{3,2,1,0:T(4,128)(2,1)}) custom-call(s32[4]{0:T(128)S(1)} %copy-done, f32[16,256]{1,0:T(8,128)S(1)} %get-tuple-element.7.projected, bf16[128,128]{1,0:T(8,128)(2,1)S(1)} %get-tuple-element.8.asked, f32[128,128]{1,0:T(8,128)S(1)} %get-tuple-element.9.best, ...), custom_call_target="tpu_custom_call" | custom-call | tf_op jit(solution)/shard_map/pallas_call | solution.py:357
Async XLA Ops:
  0.6 29.0 %copy-start = (s32[4]{0:T(128)S(1)}, s32[4]{0:T(128)}, u32[]{:S(2)}) copy-start(s32[4]{0:T(128)} %lengths.3) | copy-start | bytes 52

commit v4 on v3

--- a/solution.py
+++ b/solution.py
@@ -20,9 +20,9 @@
     hidden, base, codes, scales, queries, keys, values, lengths,
     projected, asked, best, norm, mix,
     hidden_v, queries_v, codes_v, scales_v, base_v, keys_v, values_v,
-    delta_out, delta_in, half_out, hidden_in, part_out, part_in,
+    delta_out, delta_in, half_out, hidden_in, held, part_out, part_in,
     load_sem, cache_sem, delta_send, delta_recv, pass_send, pass_recv, base_send, base_recv,
-    half_send, half_recv, spread_send, spread_recv, part_send, part_recv,
+    half_send, half_recv, held_recv, spread_send, spread_recv, part_send, part_recv, ready,
 ):
     g = lax.axis_index("group")
     s = lax.axis_index("section")
@@ -52,17 +52,21 @@
                 if i or ds or dc:
                     os, ot = lax.rem(s + ds, 2), 2 * lax.rem(chip + i, 4) + lax.rem(core + dc, 2)
                     inside.append((os * TENSORS + ot, at(g, os, ot)))
+    early = high < 2
+    mirror = WIDE * (HIGH - 1 - high) + wide
     relay = lax.rem(t + TENSORS // 2, TENSORS)
     relay_slot = 2 * lax.div(relay, 2)
-    taken = []
-    for i in turns:
-        for j in (1, 0):
-            oh = lax.rem(high + i, HIGH)
-            taken.append((i, j, oh * 2 + j, oh * WIDE + first + j))
-
+    late_cores = [at(mirror, s, 2 * lax.rem(chip + i, 4) + core) for i in turns]
     barrier = pltpu.get_barrier_semaphore()
-    for h in range(2):
-        pl.semaphore_signal(barrier, inc=1, device_id=at(2 * relay + h, s, lax.div(g, 2)), device_id_type=MESH)
+
+    @pl.when(early)
+    def _():
+        for h in range(2):
+            for og in (mirror, g):
+                pl.semaphore_signal(barrier, inc=1, device_id=at(2 * relay + h, s, lax.div(og, 2)), device_id_type=MESH)
+        for there in late_cores:
+            pl.semaphore_signal(barrier, inc=1, device_id=there, device_id_type=MESH)
+
     for _, there in inside:
         pl.semaphore_signal(barrier, inc=1, device_id=there, device_id_type=MESH)
 
@@ -100,21 +104,40 @@
         right = code[:, 128:] * turned[:, 2 * b + 1 : 2 * b + 2]
         delta_out[b] = jnp.concatenate([left, right], axis=1).astype(jnp.bfloat16)
 
-    pl.semaphore_wait(barrier, len(inside) + 2)
-
-    half_copies = []
-    for h in range(2):
-        half_copies.append(
-            pltpu.make_async_remote_copy(
-                src_ref=half_out.at[h],
-                dst_ref=hidden_in.at[high * 2 + lax.rem(wide, 2)],
-                send_sem=half_send,
-                recv_sem=half_recv,
-                device_id=at(2 * t + h, s, lax.rem(lax.div(g, 2) + TENSORS // 2, TENSORS)),
-                device_id_type=MESH,
-            )
+    pl.semaphore_wait(barrier, len(inside) + 2 + len(late_cores) * lax.div(high, 2))
+
+    @pl.when(jnp.logical_not(early))
+    def _():
+        for there in late_cores:
+            pl.semaphore_signal(ready, inc=1, device_id=there, device_id_type=MESH)
+
+    def half_copy(h, target, sem):
+        return pltpu.make_async_remote_copy(
+            src_ref=half_out.at[h],
+            dst_ref=target,
+            send_sem=half_send,
+            recv_sem=sem,
+            device_id=at(
+                WIDE * lax.div(chip * (HIGH - 1 - chip), 2) + 2 * core + h,
+                s,
+                lax.rem(lax.div(g, 2) + TENSORS // 2, TENSORS),
+            ),
+            device_id_type=MESH,
         )
-        half_copies[-1].start()
+
+    for_early = chip < 2
+    place_here = lax.rem(wide, 2)
+
+    @pl.when(for_early)
+    def _():
+        for h in range(2):
+            half_copy(h, hidden_in.at[high * 2 + place_here], half_recv).start()
+
+    @pl.when(jnp.logical_not(for_early))
+    def _():
+        for h in range(2):
+            half_copy(h, held.at[place_here], held_recv).start()
+
     for other, there in inside:
         pltpu.make_async_remote_copy(
             src_ref=delta_out.at[other],
@@ -164,20 +187,36 @@
     attend(1)
 
     here = hidden_in.at[pl.ds(relay_slot, 2)]
-    pltpu.make_async_copy(here, here, half_recv).wait()
-    spread_copies = []
-    for i in turns[:3]:
-        spread_copies.append(
-            pltpu.make_async_remote_copy(
-                src_ref=here,
-                dst_ref=here,
-                send_sem=spread_send,
-                recv_sem=spread_recv,
-                device_id=at(g, s, 2 * lax.rem(chip + i, 4) + core),
-                device_id_type=MESH,
-            )
+
+    def spread_copy(i):
+        return pltpu.make_async_remote_copy(
+            src_ref=here,
+            dst_ref=here,
+            send_sem=spread_send,
+            recv_sem=spread_recv.at[chip],
+            device_id=at(g, s, 2 * lax.rem(chip + i, 4) + core),
+            device_id_type=MESH,
         )
-        spread_copies[-1].start()
+
+    def relay_copy(there):
+        return pltpu.make_async_remote_copy(
+            src_ref=held,
+            dst_ref=here,
+            send_sem=spread_send,
+            recv_sem=spread_recv.at[chip],
+            device_id=there,
+            device_id_type=MESH,
+        )
+
+    @pl.when(early)
+    def _():
+        pltpu.make_async_copy(here, here, half_recv).wait()
+        for i in turns[:3]:
+            spread_copy(i).start()
+        pl.semaphore_wait(ready, len(late_cores))
+        pltpu.make_async_copy(held, held, held_recv).wait()
+        for there in late_cores:
+            relay_copy(there).start()
 
     mine = delta_in.at[core]
     pltpu.make_async_copy(mine, mine, delta_recv).wait()
@@ -196,15 +235,8 @@
 
     base_copy.wait_recv()
     pass_copy.wait_recv()
-    most = hidden_in.at[pl.ds(0, HALF - 2)]
-    pltpu.make_async_copy(most, most, spread_recv).wait()
-    features = hidden_in[...].reshape(HALF * rows * steps, chunk)
-    for c in range(2):
-        part = jnp.dot(features, base_v[c], preferred_element_type=jnp.float32)
-        part = part + jnp.dot(
-            features, delta_in[c].reshape(chunk, part.shape[1]), preferred_element_type=jnp.float32
-        )
-        part_out[c] = part.reshape(HALF, rows * steps, part.shape[1]).astype(jnp.bfloat16)
+    tokens = rows * steps
+    part_size = HALF // 2
 
     def send_part(c, slot, og):
         return pltpu.make_async_remote_copy(
@@ -216,39 +248,69 @@
             device_id_type=MESH,
         )
 
-    for i, j, slot, og in taken:
+    sends = []
+    for phase in range(2):
+        for from_chip in (2 - 2 * phase, 3 - 2 * phase):
+
+            @pl.when(jnp.logical_not(early & (chip == from_chip)))
+            def _():
+                pair = hidden_in.at[pl.ds(2 * ((from_chip + 2) % 4), 2)]
+                pltpu.make_async_copy(pair, pair, spread_recv.at[from_chip]).wait()
+
+        slots = pl.ds(phase * part_size, part_size)
+        features = hidden_in[slots].reshape(part_size * tokens, chunk)
         for c in range(2):
-            if i == 0:
-                local = (og == g) & (core == c)
-
-                @pl.when(local)
-                def _():
-                    pltpu.make_async_copy(part_out.at[c, slot], part_in.at[g], part_recv).start()
-
-                @pl.when(jnp.logical_not(local))
-                def _():
-                    send_part(c, slot, og).start()
-            else:
-                send_part(c, slot, og).start()
+            part = jnp.dot(features, base_v[c], preferred_element_type=jnp.float32)
+            part = part + jnp.dot(
+                features, delta_in[c].reshape(chunk, part.shape[1]), preferred_element_type=jnp.float32
+            )
+            part_out[c, slots] = part.reshape(part_size, tokens, part.shape[1]).astype(jnp.bfloat16)
+        far = lax.rem(lax.div(high + 1, 2) + 1 - phase, 2)
+        for near in range(2):
+            oh = 2 * phase + (1 - far if near else far)
+            for j in range(2):
+                for c in range(2):
+                    slot = 2 * oh + j
+                    og = WIDE * oh + first + j
+                    sends.append((c, slot, og, near))
+                    if near:
+                        local = (og == g) & (core == c)
+
+                        @pl.when(local)
+                        def _():
+                            pltpu.make_async_copy(part_out.at[c, slot], part_in.at[g], part_recv).start()
+
+                        @pl.when(jnp.logical_not(local))
+                        def _():
+                            send_part(c, slot, og).start()
+                    else:
+                        send_part(c, slot, og).start()
 
     pltpu.make_async_copy(part_in, part_in, part_recv).wait()
     projected[...] = jnp.sum(part_in[...].astype(jnp.float32), axis=0)
 
-    for copy in half_copies + spread_copies:
-        copy.wait_send()
+    for h in range(2):
+        half_copy(h, held.at[place_here], held_recv).wait_send()
+
+    @pl.when(early)
+    def _():
+        for i in turns[:3]:
+            spread_copy(i).wait_send()
+        for there in late_cores:
+            relay_copy(there).wait_send()
+
     sent = delta_out.at[pl.ds(0, BLOCKS - 1)]
     pltpu.make_async_copy(sent, sent, delta_send).wait()
     base_copy.wait_send()
     pass_copy.wait_send()
-    for i, j, slot, og in taken:
-        for c in range(2):
-            if i == 0:
-
-                @pl.when(jnp.logical_not((og == g) & (core == c)))
-                def _():
-                    send_part(c, slot, og).wait_send()
-            else:
+    for c, slot, og, near in sends:
+        if near:
+
+            @pl.when(jnp.logical_not((og == g) & (core == c)))
+            def _():
                 send_part(c, slot, og).wait_send()
+        else:
+            send_part(c, slot, og).wait_send()
 
 
 def finish(lengths, projected, asked, best, norm, mix, entries, attended, entries_v, attended_v, store_sem):
@@ -341,11 +403,13 @@
             pltpu.VMEM((2, BLOCKS, owned, width), bf16),
             pltpu.VMEM((2, tokens, chunk), bf16),
             pltpu.VMEM((HALF, tokens, chunk), bf16),
+            pltpu.VMEM((2, tokens, chunk), bf16),
             pltpu.VMEM((2, HALF, tokens, width), bf16),
             pltpu.VMEM((GROUPS, tokens, width), bf16),
             dma((5,)),
             dma((2, rows)),
-            dma, dma, dma, dma, dma, dma, dma, dma, dma, dma, dma, dma,
+            dma, dma, dma, dma, dma, dma, dma, dma, dma, dma,
+            dma((4,)), dma, dma, pltpu.SemaphoreType.REGULAR,
         ],
         compiler_params=pltpu.CompilerParams(
             collective_id=0, has_side_effects=True, vmem_limit_bytes=60 * 1024 * 1024

time: 31.4 us -> 31.5 us (level)
  no operation moved by 1% of the time
where the time goes in v4:
time: 31.5 us; the launch traced here: 31.4 us
  Pallas kernels  30.7 us (97%)
  between operations  0.66 us (2%)
    pallas_call x1, Pallas kernels, body(): pl.pallas_call(exchange, out_shape=(pltpu.VMEM((tokens, width), f32), plt...  29 us
    pallas_call x1, Pallas kernels, body(): pl.pallas_call(finish, out_shape=(jax.ShapeDtypeStruct((1, rows, steps, w...  1.7 us

profile of v4, /device:TPU:1, one launch (start us, length us, event | category | flops | bytes accessed | tf_op | source)
XLA Modules:
  0.0 31.4 jit_solution(787920689003235905)
XLA Ops:
  0.6 0.0 copy-start
  0.6 29.0 %shard_map.95 = (f32[16,256]{1,0:T(8,128)S(1)}, bf16[128,128]{1,0:T(8,128)(2,1)S(1)}, f32[128,128]{1,0:T(8,128)S(1)}, f32[128,128]{1,0:T(8,128)S(1)}, f32[128,128]{1,0:T(8,128)S(1)}) custom-call(bf16[1,4,4,1024]{3,2,1,0:T(4,128)(2,1)} %hidden.1, bf16[1,8192,256]{2,1,0:T(8,128)(2,1)} %base.1, bf16[16,32,256]{2,1,0:T(8,128)(2,1)} %codes.1, ...), custom_call_target="tpu_custom_call" | custom-call | tf_op jit(solution)/shard_map/pallas_call | solution.py:383
  29.7 0.0 copy-done
  29.7 1.7 %shard_map.96 = (bf16[1,4,4,256]{3,2,1,0:T(4,128)(2,1)}, bf16[1,4,4,1024]{3,2,1,0:T(4,128)(2,1)}) custom-call(s32[4]{0:T(128)S(1)} %copy-done, f32[16,256]{1,0:T(8,128)S(1)} %get-tuple-element.7.projected, bf16[128,128]{1,0:T(8,128)(2,1)S(1)} %get-tuple-element.8.asked, f32[128,128]{1,0:T(8,128)S(1)} %get-tuple-element.9.best, ...), custom_call_target="tpu_custom_call" | custom-call | tf_op jit(solution)/shard_map/pallas_call | solution.py:421
Async XLA Ops:
  0.6 29.0 %copy-start = (s32[4]{0:T(128)S(1)}, s32[4]{0:T(128)}, u32[]{:S(2)}) copy-start(s32[4]{0:T(128)} %lengths.3) | copy-start | bytes 52

commit v5 on v4

--- a/solution.py
+++ b/solution.py
@@ -18,7 +18,7 @@
 
 def exchange(
     hidden, base, codes, scales, queries, keys, values, lengths,
-    projected, asked, best, norm, mix,
+    projected, asked, best, norm, mix, cosine, sine,
     hidden_v, queries_v, codes_v, scales_v, base_v, keys_v, values_v,
     delta_out, delta_in, half_out, hidden_in, held, part_out, part_in,
     load_sem, cache_sem, delta_send, delta_recv, pass_send, pass_recv, base_send, base_recv,
@@ -53,19 +53,27 @@
                     os, ot = lax.rem(s + ds, 2), 2 * lax.rem(chip + i, 4) + lax.rem(core + dc, 2)
                     inside.append((os * TENSORS + ot, at(g, os, ot)))
     early = high < 2
+    takes_late = chip < 2
     mirror = WIDE * (HIGH - 1 - high) + wide
     relay = lax.rem(t + TENSORS // 2, TENSORS)
     relay_slot = 2 * lax.div(relay, 2)
+    early_high = 1 - lax.div(chip, 2)
+    early_slot = 2 * early_high + lax.rem(chip, 2)
     late_cores = [at(mirror, s, 2 * lax.rem(chip + i, 4) + core) for i in turns]
     barrier = pltpu.get_barrier_semaphore()
 
     @pl.when(early)
     def _():
-        for h in range(2):
-            for og in (mirror, g):
-                pl.semaphore_signal(barrier, inc=1, device_id=at(2 * relay + h, s, lax.div(og, 2)), device_id_type=MESH)
+        source = WIDE * early_high + first + lax.rem(chip, 2)
+        for og in (mirror, g):
+            pl.semaphore_signal(barrier, inc=1, device_id=at(source, s, lax.div(og, 2)), device_id_type=MESH)
         for there in late_cores:
             pl.semaphore_signal(barrier, inc=1, device_id=there, device_id_type=MESH)
+
+    @pl.when(takes_late)
+    def _():
+        for h in range(2):
+            pl.semaphore_signal(barrier, inc=1, device_id=at(2 * relay + h, s, lax.div(g, 2)), device_id_type=MESH)
 
     for _, there in inside:
         pl.semaphore_signal(barrier, inc=1, device_id=there, device_id_type=MESH)
@@ -108,35 +116,42 @@
 
     @pl.when(jnp.logical_not(early))
     def _():
-        for there in late_cores:
-            pl.semaphore_signal(ready, inc=1, device_id=there, device_id_type=MESH)
-
-    def half_copy(h, target, sem):
+        for i in range(4):
+            pl.semaphore_signal(ready, inc=1, device_id=at(mirror, s, 2 * i + core), device_id_type=MESH)
+
+    place_here = lax.rem(wide, 2)
+    place_there = hidden_in.at[high * 2 + place_here]
+    is_early = 1 - lax.div(high, 2)
+    relay_chip = is_early * (2 * (1 - high) + place_here) + (1 - is_early) * (high - 2)
+    turn = 1 - is_early
+
+    def half_copy(h, og, target, sem):
         return pltpu.make_async_remote_copy(
             src_ref=half_out.at[h],
             dst_ref=target,
             send_sem=half_send,
             recv_sem=sem,
-            device_id=at(
-                WIDE * lax.div(chip * (HIGH - 1 - chip), 2) + 2 * core + h,
-                s,
-                lax.rem(lax.div(g, 2) + TENSORS // 2, TENSORS),
-            ),
+            device_id=at(og, s, 2 * relay_chip + lax.div(wide, 2)),
             device_id_type=MESH,
         )
 
-    for_early = chip < 2
-    place_here = lax.rem(wide, 2)
-
-    @pl.when(for_early)
-    def _():
-        for h in range(2):
-            half_copy(h, hidden_in.at[high * 2 + place_here], half_recv).start()
-
-    @pl.when(jnp.logical_not(for_early))
-    def _():
-        for h in range(2):
-            half_copy(h, held.at[place_here], held_recv).start()
+    relayed = early & (chip >= 2)
+    via = is_early * lax.div(chip, 2)
+    half_to = [WIDE * ((1 - via) * chip + via * (HIGH - 1 - chip)) + 2 * core + h for h in range(2)]
+    stays = [(og == g) & (2 * relay_chip + lax.div(wide, 2) == t) for og in half_to]
+    for h in range(2):
+        for here_first, target, sem in (
+            (jnp.logical_not(relayed), place_there, half_recv.at[turn]),
+            (relayed, held, held_recv),
+        ):
+
+            @pl.when(here_first & stays[h])
+            def _():
+                pltpu.make_async_copy(half_out.at[h], target, sem).start()
+
+            @pl.when(here_first & jnp.logical_not(stays[h]))
+            def _():
+                half_copy(h, half_to[h], target, sem).start()
 
     for other, there in inside:
         pltpu.make_async_remote_copy(
@@ -187,13 +202,14 @@
     attend(1)
 
     here = hidden_in.at[pl.ds(relay_slot, 2)]
-
-    def spread_copy(i):
+    piece = hidden_in.at[early_slot]
+
+    def spread_copy(ref, sem, i):
         return pltpu.make_async_remote_copy(
-            src_ref=here,
-            dst_ref=here,
+            src_ref=ref,
+            dst_ref=ref,
             send_sem=spread_send,
-            recv_sem=spread_recv.at[chip],
+            recv_sem=spread_recv.at[sem],
             device_id=at(g, s, 2 * lax.rem(chip + i, 4) + core),
             device_id_type=MESH,
         )
@@ -201,22 +217,24 @@
     def relay_copy(there):
         return pltpu.make_async_remote_copy(
             src_ref=held,
-            dst_ref=here,
+            dst_ref=piece,
             send_sem=spread_send,
-            recv_sem=spread_recv.at[chip],
+            recv_sem=spread_recv.at[early_slot],
             device_id=there,
             device_id_type=MESH,
         )
 
     @pl.when(early)
     def _():
-        pltpu.make_async_copy(here, here, half_recv).wait()
+        pltpu.make_async_copy(piece, piece, half_recv.at[0]).wait()
         for i in turns[:3]:
-            spread_copy(i).start()
+            spread_copy(piece, early_slot, i).start()
         pl.semaphore_wait(ready, len(late_cores))
         pltpu.make_async_copy(held, held, held_recv).wait()
         for there in late_cores:
             relay_copy(there).start()
+
+    attend(2)
 
     mine = delta_in.at[core]
     pltpu.make_async_copy(mine, mine, delta_recv).wait()
@@ -230,13 +248,15 @@
     )
     pass_copy.start()
 
-    attend(2)
-    attend(3)
+    @pl.when(takes_late)
+    def _():
+        pltpu.make_async_copy(here, here, half_recv.at[1]).wait()
+        for i in turns[:3]:
+            spread_copy(here, 4 + chip, i).start()
 
     base_copy.wait_recv()
     pass_copy.wait_recv()
     tokens = rows * steps
-    part_size = HALF // 2
 
     def send_part(c, slot, og):
         return pltpu.make_async_remote_copy(
@@ -249,76 +269,42 @@
         )
 
     sends = []
-    for phase in range(2):
-        for from_chip in (2 - 2 * phase, 3 - 2 * phase):
-
-            @pl.when(jnp.logical_not(early & (chip == from_chip)))
+    for highs in ((0,), (1,), (2, 3)):
+        if highs[0] < 2:
+            arrivals = [(j, 1, early & (chip == 2 * (1 - highs[0]) + j), 2 * highs[0] + j) for j in range(2)]
+        else:
+            arrivals = [(2 * (oh - highs[0]), 2, chip == oh - 2, 4 + oh - 2) for oh in highs]
+        for offset, size, taken_here, sem in arrivals:
+
+            @pl.when(jnp.logical_not(taken_here))
             def _():
-                pair = hidden_in.at[pl.ds(2 * ((from_chip + 2) % 4), 2)]
-                pltpu.make_async_copy(pair, pair, spread_recv.at[from_chip]).wait()
-
-        slots = pl.ds(phase * part_size, part_size)
-        features = hidden_in[slots].reshape(part_size * tokens, chunk)
-        for c in range(2):
+                arrived = hidden_in.at[pl.ds(2 * highs[0] + offset, size)]
+                pltpu.make_async_copy(arrived, arrived, spread_recv.at[sem]).wait()
+
+        slots = pl.ds(2 * highs[0], 2 * len(highs))
+        features = hidden_in[slots].reshape(2 * len(highs) * tokens, chunk)
+        for c in (1, 0):
             part = jnp.dot(features, base_v[c], preferred_element_type=jnp.float32)
             part = part + jnp.dot(
                 features, delta_in[c].reshape(chunk, part.shape[1]), preferred_element_type=jnp.float32
             )
-            part_out[c, slots] = part.reshape(part_size, tokens, part.shape[1]).astype(jnp.bfloat16)
-        far = lax.rem(lax.div(high + 1, 2) + 1 - phase, 2)
-        for near in range(2):
-            oh = 2 * phase + (1 - far if near else far)
-            for j in range(2):
-                for c in range(2):
+            part_out[c, slots] = part.reshape(2 * len(highs), tokens, part.shape[1]).astype(jnp.bfloat16)
+            for oh in highs:
+                for j in range(2):
                     slot = 2 * oh + j
                     og = WIDE * oh + first + j
-                    sends.append((c, slot, og, near))
-                    if near:
-                        local = (og == g) & (core == c)
-
-                        @pl.when(local)
-                        def _():
-                            pltpu.make_async_copy(part_out.at[c, slot], part_in.at[g], part_recv).start()
-
-                        @pl.when(jnp.logical_not(local))
-                        def _():
-                            send_part(c, slot, og).start()
-                    else:
+                    sends.append((c, slot, og))
+                    local = (og == g) & (core == c)
+
+                    @pl.when(local)
+                    def _():
+                        pltpu.make_async_copy(part_out.at[c, slot], part_in.at[g], part_recv).start()
+
+                    @pl.when(jnp.logical_not(local))
+                    def _():
                         send_part(c, slot, og).start()
 
-    pltpu.make_async_copy(part_in, part_in, part_recv).wait()
-    projected[...] = jnp.sum(part_in[...].astype(jnp.float32), axis=0)
-
-    for h in range(2):
-        half_copy(h, held.at[place_here], held_recv).wait_send()
-
-    @pl.when(early)
-    def _():
-        for i in turns[:3]:
-            spread_copy(i).wait_send()
-        for there in late_cores:
-            relay_copy(there).wait_send()
-
-    sent = delta_out.at[pl.ds(0, BLOCKS - 1)]
-    pltpu.make_async_copy(sent, sent, delta_send).wait()
-    base_copy.wait_send()
-    pass_copy.wait_send()
-    for c, slot, og, near in sends:
-        if near:
-
-            @pl.when(jnp.logical_not((og == g) & (core == c)))
-            def _():
-                send_part(c, slot, og).wait_send()
-        else:
-            send_part(c, slot, og).wait_send()
-
-
-def finish(lengths, projected, asked, best, norm, mix, entries, attended, entries_v, attended_v, store_sem):
-    rows, steps = entries_v.shape[0], entries_v.shape[1]
-    tokens = rows * steps
-    total = asked.shape[0]
-    asks = total // rows
-    heads = asks // steps
+    attend(3)
 
     line = lax.broadcasted_iota(jnp.int32, (tokens, 128), 0)
     lane = lax.broadcasted_iota(jnp.int32, (tokens, 128), 1)
@@ -328,12 +314,52 @@
     position = (start + line % steps).astype(jnp.float32)
     frequency = jnp.exp((lane % 64).astype(jnp.float32) * (-2.0 * math.log(1000000.0) / 128))
     phase = position * frequency
-    cosine = jnp.cos(phase)
-    sine = jnp.where(lane < 64, -jnp.sin(phase), jnp.sin(phase))
+    cosine[...] = jnp.cos(phase)
+    turned_sine = jnp.sin(phase)
+    sine[...] = jnp.where(lane < 64, -turned_sine, turned_sine)
+
+    pltpu.make_async_copy(part_in, part_in, part_recv).wait()
+    projected[...] = jnp.sum(part_in[...].astype(jnp.float32), axis=0)
+
+    for h in range(2):
+
+        @pl.when(jnp.logical_not(stays[h]))
+        def _():
+            half_copy(h, g, place_there, half_recv.at[0]).wait_send()
+
+    @pl.when(takes_late)
+    def _():
+        for i in turns[:3]:
+            spread_copy(here, 4 + chip, i).wait_send()
+
+    @pl.when(early)
+    def _():
+        for i in turns[:3]:
+            spread_copy(piece, early_slot, i).wait_send()
+        for there in late_cores:
+            relay_copy(there).wait_send()
+
+    sent = delta_out.at[pl.ds(0, BLOCKS - 1)]
+    pltpu.make_async_copy(sent, sent, delta_send).wait()
+    base_copy.wait_send()
+    pass_copy.wait_send()
+    for c, slot, og in sends:
+
+        @pl.when(jnp.logical_not((og == g) & (core == c)))
+        def _():
+            send_part(c, slot, og).wait_send()
+
+
+def finish(projected, asked, best, norm, mix, cosine, sine, entries, attended, entries_v, attended_v, store_sem):
+    rows, steps = entries_v.shape[0], entries_v.shape[1]
+    tokens = rows * steps
+    total = asked.shape[0]
+    asks = total // rows
+    heads = asks // steps
 
     key = projected[:, :128]
     swapped = jnp.concatenate([key[:, 64:], key[:, :64]], axis=1)
-    fresh_key = key * cosine + swapped * sine
+    fresh_key = key * cosine[...] + swapped * sine[...]
     fresh_value = projected[:, 128:]
     for r in range(rows):
         lines = slice(r * steps, (r + 1) * steps)
@@ -388,9 +414,11 @@
             pltpu.VMEM((asks, 128), f32),
             pltpu.VMEM((asks, 128), f32),
             pltpu.VMEM((asks, 128), f32),
+            pltpu.VMEM((tokens, 128), f32),
+            pltpu.VMEM((tokens, 128), f32),
         ),
         in_specs=[anywhere] * 7 + [scalars],
-        out_specs=[fast] * 5,
+        out_specs=[fast] * 7,
         scratch_shapes=[
             pltpu.VMEM((rows, steps, slab), bf16),
             pltpu.VMEM((rows, steps, query_width), bf16),
@@ -403,13 +431,13 @@
             pltpu.VMEM((2, BLOCKS, owned, width), bf16),
             pltpu.VMEM((2, tokens, chunk), bf16),
             pltpu.VMEM((HALF, tokens, chunk), bf16),
-            pltpu.VMEM((2, tokens, chunk), bf16),
+            pltpu.VMEM((tokens, chunk), bf16),
             pltpu.VMEM((2, HALF, tokens, width), bf16),
             pltpu.VMEM((GROUPS, tokens, width), bf16),
             dma((5,)),
             dma((2, rows)),
-            dma, dma, dma, dma, dma, dma, dma, dma, dma, dma,
-            dma((4,)), dma, dma, pltpu.SemaphoreType.REGULAR,
+            dma, dma, dma, dma, dma, dma, dma,
+            dma((2,)), dma, dma, dma((6,)), dma, dma, pltpu.SemaphoreType.REGULAR,
         ],
         compiler_params=pltpu.CompilerParams(
             collective_id=0, has_side_effects=True, vmem_limit_bytes=60 * 1024 * 1024
@@ -424,7 +452,7 @@
             jax.ShapeDtypeStruct((1, rows, steps, width), bf16),
             jax.ShapeDtypeStruct((1, rows, steps, query_width), bf16),
         ),
-        in_specs=[scalars] + [fast] * 5,
+        in_specs=[fast] * 7,
         out_specs=[anywhere, anywhere],
         scratch_shapes=[
             pltpu.VMEM((rows, steps, width), bf16),
@@ -432,7 +460,7 @@
             dma((2,)),
         ],
         compiler_params=pltpu.CompilerParams(vmem_limit_bytes=8 * 1024 * 1024),
-    )(lengths, *middle)
+    )(*middle)
 
 
 def solution(mesh):

time: 31.5 us -> 29 us (0.921)
  Pallas kernels: 30.7 us -> 28.3 us
    pallas_call x1, Pallas kernels: 29 us -> 27.1 us  [body(): pl.pallas_call(exchange, out_shape=(pltpu.VMEM((tokens, width), f32), plt...]
    pallas_call x1, Pallas kernels: 1.7 us -> 1.2 us  [body(): pl.pallas_call(finish, out_shape=(jax.ShapeDtypeStruct((1, rows, steps, w...]
where the time goes in v5:
time: 29 us; the launch traced here: 28.9 us
  Pallas kernels  28.3 us (98%)
  between operations  0.64 us (2%)
    pallas_call x1, Pallas kernels, body(): pl.pallas_call(exchange, out_shape=(pltpu.VMEM((tokens, width), f32), plt...  27.1 us
    pallas_call x1, Pallas kernels, body(): pl.pallas_call(finish, out_shape=(jax.ShapeDtypeStruct((1, rows, steps, w...  1.2 us

profile of v5, /device:TPU:1, one launch (start us, length us, event | category | flops | bytes accessed | tf_op | source)
XLA Modules:
  0.0 28.9 jit_solution(4293705691851990858)
XLA Ops:
  0.6 27.1 %shard_map.95 = (f32[16,256]{1,0:T(8,128)S(1)}, bf16[128,128]{1,0:T(8,128)(2,1)S(1)}, f32[128,128]{1,0:T(8,128)S(1)}, f32[128,128]{1,0:T(8,128)S(1)}, f32[128,12...) custom-call(bf16[1,4,4,1024]{3,2,1,0:T(4,128)(2,1)} %hidden.1, bf16[1,8192,256]{2,1,0:T(8,128)(2,1)} %base.1, ...), custom_call_target="tpu_custom_call" | custom-call | tf_op jit(solution)/shard_map/pallas_call | solution.py:409
  27.7 1.2 %shard_map.96 = (bf16[1,4,4,256]{3,2,1,0:T(4,128)(2,1)}, bf16[1,4,4,1024]{3,2,1,0:T(4,128)(2,1)}) custom-call(f32[16,256]{1,0:T(8,128)S(1)} %get-tuple-element.9.projected, bf16[128,128]{1,0:T(8,128)(2,1)S(1)} %get-tuple-element.10.asked, f32[128,128]{1,0:T(8,128)S(1)} %get-tuple-element.11.best, f32[128,128]{1,0:T(8,128)S(1)} %get-tuple-element.12.norm, ...), custom_call_target="tpu_custom_call" | custom-call | tf_op jit(solution)/shard_map/pallas_call | solution.py:449

commit v6 on v5

--- a/solution.py
+++ b/solution.py
@@ -42,7 +42,6 @@
     def at(og, os, ot):
         return {"group": og, "section": os, "tensor": ot}
 
-    first = 2 * core
     sibling = 2 * chip + 1 - core
     turns = (2, 1, 3, 0)
     inside = []
@@ -53,28 +52,24 @@
                     os, ot = lax.rem(s + ds, 2), 2 * lax.rem(chip + i, 4) + lax.rem(core + dc, 2)
                     inside.append((os * TENSORS + ot, at(g, os, ot)))
     early = high < 2
-    takes_late = chip < 2
     mirror = WIDE * (HIGH - 1 - high) + wide
-    relay = lax.rem(t + TENSORS // 2, TENSORS)
-    relay_slot = 2 * lax.div(relay, 2)
-    early_high = 1 - lax.div(chip, 2)
-    early_slot = 2 * early_high + lax.rem(chip, 2)
+    early_rows = 1 - core
+    late_rows = 3 - core
+    early_wide = lax.rem(chip + 2 * core, WIDE)
+    late_wide = chip
     late_cores = [at(mirror, s, 2 * lax.rem(chip + i, 4) + core) for i in turns]
     barrier = pltpu.get_barrier_semaphore()
 
     @pl.when(early)
     def _():
-        source = WIDE * early_high + first + lax.rem(chip, 2)
         for og in (mirror, g):
-            pl.semaphore_signal(barrier, inc=1, device_id=at(source, s, lax.div(og, 2)), device_id_type=MESH)
+            there = at(WIDE * early_rows + early_wide, s, lax.div(og, 2))
+            pl.semaphore_signal(barrier, inc=1, device_id=there, device_id_type=MESH)
         for there in late_cores:
             pl.semaphore_signal(barrier, inc=1, device_id=there, device_id_type=MESH)
 
-    @pl.when(takes_late)
-    def _():
-        for h in range(2):
-            pl.semaphore_signal(barrier, inc=1, device_id=at(2 * relay + h, s, lax.div(g, 2)), device_id_type=MESH)
-
+    there = at(WIDE * late_rows + late_wide, s, lax.div(g, 2))
+    pl.semaphore_signal(barrier, inc=1, device_id=there, device_id_type=MESH)
     for _, there in inside:
         pl.semaphore_signal(barrier, inc=1, device_id=there, device_id_type=MESH)
 
@@ -119,11 +114,10 @@
         for i in range(4):
             pl.semaphore_signal(ready, inc=1, device_id=at(mirror, s, 2 * i + core), device_id_type=MESH)
 
-    place_here = lax.rem(wide, 2)
-    place_there = hidden_in.at[high * 2 + place_here]
     is_early = 1 - lax.div(high, 2)
-    relay_chip = is_early * (2 * (1 - high) + place_here) + (1 - is_early) * (high - 2)
-    turn = 1 - is_early
+    place_there = hidden_in.at[(1 - is_early) * WIDE + wide]
+    relay_core = 1 - lax.rem(high, 2)
+    relay_chip = lax.rem(wide + 2 * is_early * relay_core, WIDE)
 
     def half_copy(h, og, target, sem):
         return pltpu.make_async_remote_copy(
@@ -131,17 +125,17 @@
             dst_ref=target,
             send_sem=half_send,
             recv_sem=sem,
-            device_id=at(og, s, 2 * relay_chip + lax.div(wide, 2)),
+            device_id=at(og, s, 2 * relay_chip + relay_core),
             device_id_type=MESH,
         )
 
     relayed = early & (chip >= 2)
     via = is_early * lax.div(chip, 2)
     half_to = [WIDE * ((1 - via) * chip + via * (HIGH - 1 - chip)) + 2 * core + h for h in range(2)]
-    stays = [(og == g) & (2 * relay_chip + lax.div(wide, 2) == t) for og in half_to]
+    stays = [(og == g) & (2 * relay_chip + relay_core == t) for og in half_to]
     for h in range(2):
         for here_first, target, sem in (
-            (jnp.logical_not(relayed), place_there, half_recv.at[turn]),
+            (jnp.logical_not(relayed), place_there, half_recv.at[1 - is_early]),
             (relayed, held, held_recv),
         ):
 
@@ -201,13 +195,13 @@
     attend(0)
     attend(1)
 
-    here = hidden_in.at[pl.ds(relay_slot, 2)]
-    piece = hidden_in.at[early_slot]
-
-    def spread_copy(ref, sem, i):
+    early_piece = hidden_in.at[early_wide]
+    late_piece = hidden_in.at[WIDE + late_wide]
+
+    def spread_copy(piece, sem, i):
         return pltpu.make_async_remote_copy(
-            src_ref=ref,
-            dst_ref=ref,
+            src_ref=piece,
+            dst_ref=piece,
             send_sem=spread_send,
             recv_sem=spread_recv.at[sem],
             device_id=at(g, s, 2 * lax.rem(chip + i, 4) + core),
@@ -217,18 +211,18 @@
     def relay_copy(there):
         return pltpu.make_async_remote_copy(
             src_ref=held,
-            dst_ref=piece,
+            dst_ref=early_piece,
             send_sem=spread_send,
-            recv_sem=spread_recv.at[early_slot],
+            recv_sem=spread_recv.at[early_wide],
             device_id=there,
             device_id_type=MESH,
         )
 
     @pl.when(early)
     def _():
-        pltpu.make_async_copy(piece, piece, half_recv.at[0]).wait()
+        pltpu.make_async_copy(early_piece, early_piece, half_recv.at[0]).wait()
         for i in turns[:3]:
-            spread_copy(piece, early_slot, i).start()
+            spread_copy(early_piece, early_wide, i).start()
         pl.semaphore_wait(ready, len(late_cores))
         pltpu.make_async_copy(held, held, held_recv).wait()
         for there in late_cores:
@@ -248,11 +242,9 @@
     )
     pass_copy.start()
 
-    @pl.when(takes_late)
-    def _():
-        pltpu.make_async_copy(here, here, half_recv.at[1]).wait()
-        for i in turns[:3]:
-            spread_copy(here, 4 + chip, i).start()
+    pltpu.make_async_copy(late_piece, late_piece, half_recv.at[1]).wait()
+    for i in turns[:3]:
+        spread_copy(late_piece, WIDE + late_wide, i).start()
 
     base_copy.wait_recv()
     pass_copy.wait_recv()
@@ -269,40 +261,36 @@
         )
 
     sends = []
-    for highs in ((0,), (1,), (2, 3)):
-        if highs[0] < 2:
-            arrivals = [(j, 1, early & (chip == 2 * (1 - highs[0]) + j), 2 * highs[0] + j) for j in range(2)]
-        else:
-            arrivals = [(2 * (oh - highs[0]), 2, chip == oh - 2, 4 + oh - 2) for oh in highs]
-        for offset, size, taken_here, sem in arrivals:
+    for phase, oh in enumerate((early_rows, late_rows)):
+        for j in range(WIDE):
+            taken_here = (early & (early_wide == j)) if phase == 0 else (late_wide == j)
 
             @pl.when(jnp.logical_not(taken_here))
             def _():
-                arrived = hidden_in.at[pl.ds(2 * highs[0] + offset, size)]
-                pltpu.make_async_copy(arrived, arrived, spread_recv.at[sem]).wait()
-
-        slots = pl.ds(2 * highs[0], 2 * len(highs))
-        features = hidden_in[slots].reshape(2 * len(highs) * tokens, chunk)
+                piece = hidden_in.at[phase * WIDE + j]
+                pltpu.make_async_copy(piece, piece, spread_recv.at[phase * WIDE + j]).wait()
+
+        slots = pl.ds(phase * WIDE, WIDE)
+        features = hidden_in[slots].reshape(WIDE * tokens, chunk)
         for c in (1, 0):
             part = jnp.dot(features, base_v[c], preferred_element_type=jnp.float32)
             part = part + jnp.dot(
                 features, delta_in[c].reshape(chunk, part.shape[1]), preferred_element_type=jnp.float32
             )
-            part_out[c, slots] = part.reshape(2 * len(highs), tokens, part.shape[1]).astype(jnp.bfloat16)
-            for oh in highs:
-                for j in range(2):
-                    slot = 2 * oh + j
-                    og = WIDE * oh + first + j
-                    sends.append((c, slot, og))
-                    local = (og == g) & (core == c)
-
-                    @pl.when(local)
-                    def _():
-                        pltpu.make_async_copy(part_out.at[c, slot], part_in.at[g], part_recv).start()
-
-                    @pl.when(jnp.logical_not(local))
-                    def _():
-                        send_part(c, slot, og).start()
+            part_out[c, slots] = part.reshape(WIDE, tokens, part.shape[1]).astype(jnp.bfloat16)
+            for j in range(WIDE):
+                slot = phase * WIDE + j
+                og = WIDE * oh + j
+                sends.append((c, slot, og))
+                local = (og == g) & (core == c)
+
+                @pl.when(local)
+                def _():
+                    pltpu.make_async_copy(part_out.at[c, slot], part_in.at[g], part_recv).start()
+
+                @pl.when(jnp.logical_not(local))
+                def _():
+                    send_part(c, slot, og).start()
 
     attend(3)
 
@@ -318,24 +306,19 @@
     turned_sine = jnp.sin(phase)
     sine[...] = jnp.where(lane < 64, -turned_sine, turned_sine)
 
-    pltpu.make_async_copy(part_in, part_in, part_recv).wait()
-    projected[...] = jnp.sum(part_in[...].astype(jnp.float32), axis=0)
-
     for h in range(2):
 
         @pl.when(jnp.logical_not(stays[h]))
         def _():
             half_copy(h, g, place_there, half_recv.at[0]).wait_send()
 
-    @pl.when(takes_late)
-    def _():
-        for i in turns[:3]:
-            spread_copy(here, 4 + chip, i).wait_send()
+    for i in turns[:3]:
+        spread_copy(late_piece, WIDE + late_wide, i).wait_send()
 
     @pl.when(early)
     def _():
         for i in turns[:3]:
-            spread_copy(piece, early_slot, i).wait_send()
+            spread_copy(early_piece, early_wide, i).wait_send()
         for there in late_cores:
             relay_copy(there).wait_send()
 
@@ -348,6 +331,9 @@
         @pl.when(jnp.logical_not((og == g) & (core == c)))
         def _():
             send_part(c, slot, og).wait_send()
+
+    pltpu.make_async_copy(part_in, part_in, part_recv).wait()
+    projected[...] = jnp.sum(part_in[...].astype(jnp.float32), axis=0)
 
 
 def finish(projected, asked, best, norm, mix, cosine, sine, entries, attended, entries_v, attended_v, store_sem):
@@ -437,7 +423,7 @@
             dma((5,)),
             dma((2, rows)),
             dma, dma, dma, dma, dma, dma, dma,
-            dma((2,)), dma, dma, dma((6,)), dma, dma, pltpu.SemaphoreType.REGULAR,
+            dma((2,)), dma, dma, dma((2 * WIDE,)), dma, dma, pltpu.SemaphoreType.REGULAR,
         ],
         compiler_params=pltpu.CompilerParams(
             collective_id=0, has_side_effects=True, vmem_limit_bytes=60 * 1024 * 1024

time: 29 us -> 27.8 us (0.959)
  the two profiles are of different devices: /device:TPU:1 before, /device:TPU:32 now
where the time goes in v6:
time: 27.8 us; the launch traced here: 27.7 us
  Pallas kernels  27 us (97%)
  between operations  0.64 us (2%)
    pallas_call x1, Pallas kernels, body(): pl.pallas_call(exchange, out_shape=(pltpu.VMEM((tokens, width), f32), plt...  25.8 us
    pallas_call x1, Pallas kernels, body(): pl.pallas_call(finish, out_shape=(jax.ShapeDtypeStruct((1, rows, steps, w...  1.2 us

profile of v6, /device:TPU:32, one launch (start us, length us, event | category | flops | bytes accessed | tf_op | source)
XLA Modules:
  0.0 27.7 jit_solution(8919835041432615771)
XLA Ops:
  0.6 25.8 %shard_map.95 = (f32[16,256]{1,0:T(8,128)S(1)}, bf16[128,128]{1,0:T(8,128)(2,1)S(1)}, f32[128,128]{1,0:T(8,128)S(1)}, f32[128,128]{1,0:T(8,128)S(1)}, f32[128,12...) custom-call(bf16[1,4,4,1024]{3,2,1,0:T(4,128)(2,1)} %hidden.1, bf16[1,8192,256]{2,1,0:T(8,128)(2,1)} %base.1, ...), custom_call_target="tpu_custom_call" | custom-call | tf_op jit(solution)/shard_map/pallas_call | solution.py:395
  26.5 1.2 %shard_map.96 = (bf16[1,4,4,256]{3,2,1,0:T(4,128)(2,1)}, bf16[1,4,4,1024]{3,2,1,0:T(4,128)(2,1)}) custom-call(f32[16,256]{1,0:T(8,128)S(1)} %get-tuple-element.9.projected, bf16[128,128]{1,0:T(8,128)(2,1)S(1)} %get-tuple-element.10.asked, f32[128,128]{1,0:T(8,128)S(1)} %get-tuple-element.11.best, f32[128,128]{1,0:T(8,128)S(1)} %get-tuple-element.12.norm, ...), custom_call_target="tpu_custom_call" | custom-call | tf_op jit(solution)/shard_map/pallas_call | solution.py:435

commit v7 on v6

--- a/solution.py
+++ b/solution.py
@@ -57,16 +57,27 @@
     late_rows = 3 - core
     early_wide = lax.rem(chip + 2 * core, WIDE)
     late_wide = chip
-    late_cores = [at(mirror, s, 2 * lax.rem(chip + i, 4) + core) for i in turns]
+    relays = ((early & (s * core * high == 0), mirror), ((high == 0) & (s * core == 1), 2 * WIDE + wide))
+
+    def late_cores(og):
+        return [at(og, s, 2 * lax.rem(chip + i, 4) + core) for i in turns]
+
     barrier = pltpu.get_barrier_semaphore()
+
+    def early_source(og):
+        return at(WIDE * early_rows + early_wide, s, lax.div(og, 2))
+
+    for does, og in relays:
+
+        @pl.when(does)
+        def _():
+            pl.semaphore_signal(barrier, inc=1, device_id=early_source(og), device_id_type=MESH)
+            for there in late_cores(og):
+                pl.semaphore_signal(barrier, inc=1, device_id=there, device_id_type=MESH)
 
     @pl.when(early)
     def _():
-        for og in (mirror, g):
-            there = at(WIDE * early_rows + early_wide, s, lax.div(og, 2))
-            pl.semaphore_signal(barrier, inc=1, device_id=there, device_id_type=MESH)
-        for there in late_cores:
-            pl.semaphore_signal(barrier, inc=1, device_id=there, device_id_type=MESH)
+        pl.semaphore_signal(barrier, inc=1, device_id=early_source(g), device_id_type=MESH)
 
     there = at(WIDE * late_rows + late_wide, s, lax.div(g, 2))
     pl.semaphore_signal(barrier, inc=1, device_id=there, device_id_type=MESH)
@@ -107,12 +118,15 @@
         right = code[:, 128:] * turned[:, 2 * b + 1 : 2 * b + 2]
         delta_out[b] = jnp.concatenate([left, right], axis=1).astype(jnp.bfloat16)
 
-    pl.semaphore_wait(barrier, len(inside) + 2 + len(late_cores) * lax.div(high, 2))
+    pl.semaphore_wait(barrier, len(inside) + 2 + 4 * lax.div(high, 2))
 
     @pl.when(jnp.logical_not(early))
     def _():
+        which = s * core * (HIGH - 1 - high)
+        og = WIDE * (HIGH - 1 - high) * (1 - s * core) + wide
         for i in range(4):
-            pl.semaphore_signal(ready, inc=1, device_id=at(mirror, s, 2 * i + core), device_id_type=MESH)
+            there = at(og, s, 2 * i + core)
+            pl.semaphore_signal(ready.at[which], inc=1, device_id=there, device_id_type=MESH)
 
     is_early = 1 - lax.div(high, 2)
     place_there = hidden_in.at[(1 - is_early) * WIDE + wide]
@@ -131,12 +145,13 @@
 
     relayed = early & (chip >= 2)
     via = is_early * lax.div(chip, 2)
-    half_to = [WIDE * ((1 - via) * chip + via * (HIGH - 1 - chip)) + 2 * core + h for h in range(2)]
+    which_held = via * s * (1 - high) * (HIGH - 1 - chip)
+    half_to = [WIDE * ((1 - via) * chip + via * (1 - s * (1 - high)) * (HIGH - 1 - chip)) + 2 * core + h for h in range(2)]
     stays = [(og == g) & (2 * relay_chip + relay_core == t) for og in half_to]
     for h in range(2):
         for here_first, target, sem in (
             (jnp.logical_not(relayed), place_there, half_recv.at[1 - is_early]),
-            (relayed, held, held_recv),
+            (relayed, held.at[which_held], held_recv.at[which_held]),
         ):
 
             @pl.when(here_first & stays[h])
@@ -208,9 +223,9 @@
             device_id_type=MESH,
         )
 
-    def relay_copy(there):
+    def relay_copy(k, there):
         return pltpu.make_async_remote_copy(
-            src_ref=held,
+            src_ref=held.at[k],
             dst_ref=early_piece,
             send_sem=spread_send,
             recv_sem=spread_recv.at[early_wide],
@@ -223,10 +238,16 @@
         pltpu.make_async_copy(early_piece, early_piece, half_recv.at[0]).wait()
         for i in turns[:3]:
             spread_copy(early_piece, early_wide, i).start()
-        pl.semaphore_wait(ready, len(late_cores))
-        pltpu.make_async_copy(held, held, held_recv).wait()
-        for there in late_cores:
-            relay_copy(there).start()
+
+    for k in (1, 0):
+        does, og = relays[k]
+
+        @pl.when(does)
+        def _():
+            pl.semaphore_wait(ready.at[k], 4)
+            pltpu.make_async_copy(held.at[k], held.at[k], held_recv.at[k]).wait()
+            for there in late_cores(og):
+                relay_copy(k, there).start()
 
     attend(2)
 
@@ -261,8 +282,9 @@
         )
 
     sends = []
-    for phase, oh in enumerate((early_rows, late_rows)):
-        for j in range(WIDE):
+    for phase, taken in ((0, (0, 1)), (0, (2, 3)), (1, (0, 1, 2, 3))):
+        oh = (early_rows, late_rows)[phase]
+        for j in taken:
             taken_here = (early & (early_wide == j)) if phase == 0 else (late_wide == j)
 
             @pl.when(jnp.logical_not(taken_here))
@@ -270,15 +292,15 @@
                 piece = hidden_in.at[phase * WIDE + j]
                 pltpu.make_async_copy(piece, piece, spread_recv.at[phase * WIDE + j]).wait()
 
-        slots = pl.ds(phase * WIDE, WIDE)
-        features = hidden_in[slots].reshape(WIDE * tokens, chunk)
+        slots = pl.ds(phase * WIDE + taken[0], len(taken))
+        features = hidden_in[slots].reshape(len(taken) * tokens, chunk)
         for c in (1, 0):
             part = jnp.dot(features, base_v[c], preferred_element_type=jnp.float32)
             part = part + jnp.dot(
                 features, delta_in[c].reshape(chunk, part.shape[1]), preferred_element_type=jnp.float32
             )
-            part_out[c, slots] = part.reshape(WIDE, tokens, part.shape[1]).astype(jnp.bfloat16)
-            for j in range(WIDE):
+            part_out[c, slots] = part.reshape(len(taken), tokens, part.shape[1]).astype(jnp.bfloat16)
+            for j in taken:
                 slot = phase * WIDE + j
                 og = WIDE * oh + j
                 sends.append((c, slot, og))
@@ -319,8 +341,13 @@
     def _():
         for i in turns[:3]:
             spread_copy(early_piece, early_wide, i).wait_send()
-        for there in late_cores:
-            relay_copy(there).wait_send()
+
+    for k, (does, og) in enumerate(relays):
+
+        @pl.when(does)
+        def _():
+            for there in late_cores(og):
+                relay_copy(k, there).wait_send()
 
     sent = delta_out.at[pl.ds(0, BLOCKS - 1)]
     pltpu.make_async_copy(sent, sent, delta_send).wait()
@@ -417,13 +444,13 @@
             pltpu.VMEM((2, BLOCKS, owned, width), bf16),
             pltpu.VMEM((2, tokens, chunk), bf16),
             pltpu.VMEM((HALF, tokens, chunk), bf16),
-            pltpu.VMEM((tokens, chunk), bf16),
+            pltpu.VMEM((2, tokens, chunk), bf16),
             pltpu.VMEM((2, HALF, tokens, width), bf16),
             pltpu.VMEM((GROUPS, tokens, width), bf16),
             dma((5,)),
             dma((2, rows)),
             dma, dma, dma, dma, dma, dma, dma,
-            dma((2,)), dma, dma, dma((2 * WIDE,)), dma, dma, pltpu.SemaphoreType.REGULAR,
+            dma((2,)), dma((2,)), dma, dma((2 * WIDE,)), dma, dma, pltpu.SemaphoreType.REGULAR((2,)),
         ],
         compiler_params=pltpu.CompilerParams(
             collective_id=0, has_side_effects=True, vmem_limit_bytes=60 * 1024 * 1024

time: 27.8 us -> 27.3 us (0.982)
  the two profiles are of different devices: /device:TPU:32 before, /device:TPU:1 now
where the time goes in v7:
time: 27.3 us; the launch traced here: 27.2 us
  Pallas kernels  26.5 us (97%)
  between operations  0.64 us (2%)
    pallas_call x1, Pallas kernels, body(): pl.pallas_call(exchange, out_shape=(pltpu.VMEM((tokens, width), f32), plt...  25.3 us
    pallas_call x1, Pallas kernels, body(): pl.pallas_call(finish, out_shape=(jax.ShapeDtypeStruct((1, rows, steps, w...  1.2 us

profile of v7, /device:TPU:1, one launch (start us, length us, event | category | flops | bytes accessed | tf_op | source)
XLA Modules:
  0.0 27.2 jit_solution(16451464979222794206)
XLA Ops:
  0.6 25.3 %shard_map.95 = (f32[16,256]{1,0:T(8,128)S(1)}, bf16[128,128]{1,0:T(8,128)(2,1)S(1)}, f32[128,128]{1,0:T(8,128)S(1)}, f32[128,128]{1,0:T(8,128)S(1)}, f32[128,12...) custom-call(bf16[1,4,4,1024]{3,2,1,0:T(4,128)(2,1)} %hidden.1, bf16[1,8192,256]{2,1,0:T(8,128)(2,1)} %base.1, ...), custom_call_target="tpu_custom_call" | custom-call | tf_op jit(solution)/shard_map/pallas_call | solution.py:422
  26.0 1.2 %shard_map.96 = (bf16[1,4,4,256]{3,2,1,0:T(4,128)(2,1)}, bf16[1,4,4,1024]{3,2,1,0:T(4,128)(2,1)}) custom-call(f32[16,256]{1,0:T(8,128)S(1)} %get-tuple-element.9.projected, bf16[128,128]{1,0:T(8,128)(2,1)S(1)} %get-tuple-element.10.asked, f32[128,128]{1,0:T(8,128)S(1)} %get-tuple-element.11.best, f32[128,128]{1,0:T(8,128)S(1)} %get-tuple-element.12.norm, ...), custom_call_target="tpu_custom_call" | custom-call | tf_op jit(solution)/shard_map/pallas_call | solution.py:462

commit v8 on v7

--- a/solution.py
+++ b/solution.py
@@ -263,10 +263,6 @@
     )
     pass_copy.start()
 
-    pltpu.make_async_copy(late_piece, late_piece, half_recv.at[1]).wait()
-    for i in turns[:3]:
-        spread_copy(late_piece, WIDE + late_wide, i).start()
-
     base_copy.wait_recv()
     pass_copy.wait_recv()
     tokens = rows * steps
@@ -281,9 +277,18 @@
             device_id_type=MESH,
         )
 
+    def pass_late():
+        pltpu.make_async_copy(late_piece, late_piece, half_recv.at[1]).wait()
+        for i in turns[:3]:
+            spread_copy(late_piece, WIDE + late_wide, i).start()
+
+    pl.when(jnp.logical_not(early))(pass_late)
     sends = []
     for phase, taken in ((0, (0, 1)), (0, (2, 3)), (1, (0, 1, 2, 3))):
         oh = (early_rows, late_rows)[phase]
+        if taken == (2, 3):
+            pl.when(early)(pass_late)
+
         for j in taken:
             taken_here = (early & (early_wide == j)) if phase == 0 else (late_wide == j)
 

time: 27.3 us -> 27.4 us (level)
  no operation moved by 1% of the time
where the time goes in v8:
time: 27.4 us; the launch traced here: 27.1 us
  Pallas kernels  26.5 us (97%)
  between operations  0.64 us (2%)
    pallas_call x1, Pallas kernels, body(): pl.pallas_call(exchange, out_shape=(pltpu.VMEM((tokens, width), f32), plt...  25.3 us
    pallas_call x1, Pallas kernels, body(): pl.pallas_call(finish, out_shape=(jax.ShapeDtypeStruct((1, rows, steps, w...  1.2 us

profile of v8, /device:TPU:1, one launch (start us, length us, event | category | flops | bytes accessed | tf_op | source)
XLA Modules:
  0.0 27.1 jit_solution(16612214165880882490)
XLA Ops:
  0.6 25.3 %shard_map.95 = (f32[16,256]{1,0:T(8,128)S(1)}, bf16[128,128]{1,0:T(8,128)(2,1)S(1)}, f32[128,128]{1,0:T(8,128)S(1)}, f32[128,128]{1,0:T(8,128)S(1)}, f32[128,12...) custom-call(bf16[1,4,4,1024]{3,2,1,0:T(4,128)(2,1)} %hidden.1, bf16[1,8192,256]{2,1,0:T(8,128)(2,1)} %base.1, ...), custom_call_target="tpu_custom_call" | custom-call | tf_op jit(solution)/shard_map/pallas_call | solution.py:427
  25.9 1.2 %shard_map.96 = (bf16[1,4,4,256]{3,2,1,0:T(4,128)(2,1)}, bf16[1,4,4,1024]{3,2,1,0:T(4,128)(2,1)}) custom-call(f32[16,256]{1,0:T(8,128)S(1)} %get-tuple-element.9.projected, bf16[128,128]{1,0:T(8,128)(2,1)S(1)} %get-tuple-element.10.asked, f32[128,128]{1,0:T(8,128)S(1)} %get-tuple-element.11.best, f32[128,128]{1,0:T(8,128)S(1)} %get-tuple-element.12.norm, ...), custom_call_target="tpu_custom_call" | custom-call | tf_op jit(solution)/shard_map/pallas_call | solution.py:467
